TPU v7x, 32 devices: a whole 2x2x4 slice. The times are simulated.
32 devices in a mesh: dp: 2 (over core), expert: 16 (over z, y, x).
Axes of the slice: x: 2, y: 2, z: 4, core: 2. Of those that a mesh axis runs over, the one named last changes fastest.
Arguments:
- tokens: bfloat16 [4096, 768], P(('dp', 'expert')), may hold values from -6 to 6
- cotangent: bfloat16 [4096, 768], P(('dp', 'expert')), may hold values from -6 to 6
- segment_ids: int32 [32, 128], P(('dp', 'expert')), may hold values from 0 to 7, never falling along the last dimension, each value on 1 to 32 neighbouring positions
- routes: int32 [4096, 1], P(('dp', 'expert')), may hold values from 0 to 7; in each aligned block of 128 rows (0 to 127, 128 to 255, ...) at most 32 rows name the same one
- bucket_table: int32 [257], replicated, may hold values from 0 to 31
- mixer_weight: bfloat16 [3072, 768], P(('dp', 'expert'))
- rel_bias: float32 [32, 12], replicated, may hold values from -4 to 4
- gain_attn: float32 [768], replicated, may hold values from 0.5 to 1.5
- gain_ffn: float32 [768], replicated, may hold values from 0.5 to 1.5
- router_weight: bfloat16 [768, 8], replicated, may hold values from -0.15625 to 0.15625
- expert_in: bfloat16 [16, 768, 1536], P('expert', 'dp'), may hold values from -0.21875 to 0.21875
- expert_out: bfloat16 [16, 768, 1536], P('expert', 'dp'), may hold values from -0.875 to 0.875
Outputs:
- mixed: bfloat16 [4096, 768], P(('dp', 'expert'))
- tokens_grad: float32 [4096, 768], P(('dp', 'expert'))
- mixer_grad: float32 [3072, 768], P(('dp', 'expert'))
- rel_bias_grad: float32 [32, 12], replicated
- gain_attn_grad: float32 [768], replicated
- gain_ffn_grad: float32 [768], replicated
- router_grad: float32 [768, 8], replicated
- expert_in_grad: float32 [16, 768, 1536], P('expert', 'dp')
- expert_out_grad: float32 [16, 768, 1536], P('expert', 'dp')
Inputs may be any that keep to these rules, and one draw needn't show every extreme that they name: `routes`: in each sequence's 128 tokens, no expert is chosen more than 32 times; some expert is chosen exactly 32 times in some sequence. `segment_ids`: never falling along a sequence; a document has at most 32 tokens.
All inputs are finite; a program needn't handle non-finite values.
Results may differ from a plain program's by a relative error of at most 0.012.
The roundings to bfloat16 on the way count: a program that leaves them out, or rounds other values in their place, can miss the bound.
Values may be sent and summed in bfloat16 or wider, within the bound.
A program may use at most 128 MiB of HBM per device.

v0:
```python
import jax
import jax.numpy as jnp
from jax import lax
from jax.sharding import PartitionSpec as P


def rms_scale(rows, gain):
    inverse = lax.rsqrt(jnp.mean(rows * rows, axis=-1, keepdims=True) + 1e-06)
    return rows * inverse * gain


def gate_value(logits, chosen):
    return jnp.sum(jax.nn.softmax(logits, axis=-1) * chosen, axis=-1)


def tanh_gelu(values):
    return jax.nn.gelu(values, approximate=True)


def contract_first(left, right):
    return lax.dot_general(
        left, right, (((0,), (0,)), ((), ())), preferred_element_type=jnp.float32
    )


def contract_last(left, right):
    return lax.dot_general(
        left, right, (((1,), (1,)), ((), ())), preferred_element_type=jnp.float32
    )


def select_rows(place, values):
    return jnp.dot(place, values, precision=lax.Precision.HIGHEST)


def deliver(buffer, experts, capacity, width):
    doubled = jnp.broadcast_to(
        buffer.reshape(experts, 1, capacity, width), (experts, 2, capacity, width)
    )
    return lax.all_to_all(
        doubled.reshape(2 * experts * capacity, width),
        "expert",
        split_axis=0,
        concat_axis=0,
        tiled=True,
    )


def collect(results, experts, capacity, width):
    returned = lax.all_to_all(results, "expert", split_axis=0, concat_axis=0, tiled=True)
    return jnp.sum(returned.reshape(experts, 2, capacity, width), axis=1).reshape(
        experts * capacity, width
    )


def shards(
    tokens,
    cotangent,
    segment_ids,
    routes,
    bucket_table,
    mixer_weight,
    rel_bias,
    gain_attn,
    gain_ffn,
    router_weight,
    expert_in,
    expert_out,
):
    f32 = jnp.float32
    bf16 = jnp.bfloat16
    highest = lax.Precision.HIGHEST
    count, width = tokens.shape
    buckets, heads = rel_bias.shape
    head_dim = width // heads
    experts = router_weight.shape[1]
    capacity = 2 * max(1, count // experts)
    reach = (bucket_table.shape[0] - 1) // 2
    scale = head_dim ** (-0.5)
    mixer = lax.all_gather(mixer_weight, ("dp", "expert"), axis=0, tiled=True)
    inner_all, outer_all = (
        lax.all_gather(expert_in, "dp", axis=1, tiled=True),
        lax.all_gather(expert_out, "dp", axis=1, tiled=True),
    )
    w_inner = inner_all[0]
    w_outer = outer_all[0]
    xf = tokens.astype(f32)
    norm_one, norm_one_back = jax.vjp(rms_scale, xf, gain_attn)
    normed_one = norm_one.astype(bf16)
    qkv = contract_last(normed_one, mixer[: 3 * width]).astype(bf16)
    queries = qkv[:, :width].reshape(count, heads, head_dim)
    keys = qkv[:, width : 2 * width].reshape(count, heads, head_dim)
    values = qkv[:, 2 * width :].reshape(count, heads, head_dim)
    spacing = jnp.arange(count)[None, :] - jnp.arange(count)[:, None]
    bucket = jnp.take(bucket_table, jnp.clip(spacing, -reach, reach) + reach)
    bucket_hot = (bucket[:, :, None] == jnp.arange(buckets)[None, None, :]).astype(f32)
    bias = jnp.einsum("ijb,bh->hij", bucket_hot, rel_bias, precision=highest)
    segment = segment_ids[0]
    same = (segment[:, None] == segment[None, :])[None]
    scores = jnp.einsum("ihd,jhd->hij", queries, keys, preferred_element_type=f32) * scale + bias
    scores = jnp.where(same, scores, -1e30)
    peak = jnp.max(scores, axis=-1, keepdims=True)
    weights = jnp.exp(scores - peak)
    probs = weights / jnp.sum(weights, axis=-1, keepdims=True)
    probs_low = probs.astype(bf16)
    attended = (
        jnp.einsum("hij,jhd->ihd", probs_low, values, preferred_element_type=f32)
        .astype(bf16)
        .reshape(count, width)
    )
    x_mid = xf + contract_last(attended, mixer[3 * width :])
    norm_two, norm_two_back = jax.vjp(rms_scale, x_mid, gain_ffn)
    normed_two = norm_two.astype(bf16)
    logits = jnp.dot(normed_two, router_weight, preferred_element_type=f32)
    route = routes[:, 0]
    chosen = (route[:, None] == jnp.arange(experts)[None, :]).astype(f32)
    gate, gate_back = jax.vjp(lambda scores_in: gate_value(scores_in, chosen), logits)
    earlier = jnp.cumsum(chosen, axis=0) - chosen
    slot = jnp.sum(earlier * chosen, axis=1).astype(jnp.int32)
    column = route * capacity + slot
    place_hot = column[:, None] == jnp.arange(experts * capacity)[None, :]
    place = place_hot.astype(bf16)
    place_wide = place_hot.astype(f32)
    buffer = contract_first(place, normed_two).astype(bf16)
    arrived = deliver(buffer, experts, capacity, width)
    hidden = jnp.dot(arrived, w_inner, preferred_element_type=f32)
    active, active_back = jax.vjp(tanh_gelu, hidden)
    active_low = active.astype(bf16)
    partial_rows = contract_last(active_low, w_outer)
    expert_rows = collect(partial_rows, experts, capacity, width)
    expert_tok = select_rows(place_wide, expert_rows)
    mixed = (x_mid + gate[:, None] * expert_tok).astype(bf16)
    upstream = cotangent.astype(f32)
    gate_grad = jnp.sum(upstream * expert_tok, axis=1)
    expert_grad_tok = (gate[:, None] * upstream).astype(bf16)
    grad_arrived = deliver(
        contract_first(place, expert_grad_tok).astype(bf16), experts, capacity, width
    )
    active_grad = jnp.dot(grad_arrived, w_outer, preferred_element_type=f32)
    hidden_grad = active_back(active_grad)[0].astype(bf16)
    input_part = contract_last(hidden_grad, w_inner)
    input_rows = collect(input_part, experts, capacity, width)
    outer_grad = contract_first(grad_arrived, active_low)
    inner_grad = contract_first(arrived, hidden_grad)
    inner_share, outer_share = (
        lax.psum_scatter(inner_grad[None], "dp", scatter_dimension=1, tiled=True),
        lax.psum_scatter(outer_grad[None], "dp", scatter_dimension=1, tiled=True),
    )
    logit_grad = gate_back(gate_grad)[0].astype(bf16)
    router_local = contract_first(normed_two, logit_grad)
    norm_two_grad = select_rows(place_wide, input_rows) + contract_last(logit_grad, router_weight)
    mid_part, gain_ffn_local = norm_two_back(norm_two_grad)
    mid_grad = upstream + mid_part
    branch_grad = mid_grad.astype(bf16)
    out_block_grad = contract_first(branch_grad, attended)
    attended_grad = (
        jnp.dot(branch_grad, mixer[3 * width :], preferred_element_type=f32)
        .astype(bf16)
        .reshape(count, heads, head_dim)
    )
    prob_grad = jnp.einsum("ihd,jhd->hij", attended_grad, values, preferred_element_type=f32)
    score_grad = probs * (prob_grad - jnp.sum(prob_grad * probs, axis=-1, keepdims=True))
    bias_local = jnp.einsum("hij,ijb->bh", score_grad, bucket_hot, precision=highest)
    product_grad = (score_grad * scale).astype(bf16)
    query_grad = jnp.einsum("hij,jhd->ihd", product_grad, keys, preferred_element_type=f32).astype(
        bf16
    )
    key_grad = jnp.einsum("hij,ihd->jhd", product_grad, queries, preferred_element_type=f32).astype(
        bf16
    )
    value_grad = jnp.einsum(
        "hij,ihd->jhd", probs_low, attended_grad, preferred_element_type=f32
    ).astype(bf16)
    qkv_grad = jnp.concatenate(
        [
            query_grad.reshape(count, width),
            key_grad.reshape(count, width),
            value_grad.reshape(count, width),
        ],
        axis=1,
    )
    in_block_grad = contract_first(qkv_grad, normed_one)
    norm_one_grad = jnp.dot(qkv_grad, mixer[: 3 * width], preferred_element_type=f32)
    input_part_one, gain_attn_local = norm_one_back(norm_one_grad)
    tokens_grad = mid_grad + input_part_one
    mixer_grad = lax.psum_scatter(
        jnp.concatenate([in_block_grad, out_block_grad], axis=0),
        ("dp", "expert"),
        scatter_dimension=0,
        tiled=True,
    )
    bias_sum, attn_gain_sum, ffn_gain_sum, router_sum = lax.psum(
        (bias_local, gain_attn_local, gain_ffn_local, router_local), ("dp", "expert")
    )
    return (
        mixed,
        tokens_grad,
        mixer_grad,
        bias_sum,
        attn_gain_sum,
        ffn_gain_sum,
        router_sum,
        inner_share,
        outer_share,
    )


def solution(mesh):
    placed = (
        P(("dp", "expert"), None),
        P(("dp", "expert"), None),
        P(("dp", "expert"), None),
        P(("dp", "expert"), None),
        P(),
        P(("dp", "expert"), None),
        P(),
        P(),
        P(),
        P(),
        P("expert", "dp", None),
        P("expert", "dp", None),
    )
    return jax.shard_map(
        shards,
        mesh=mesh,
        in_specs=placed,
        out_specs=(
            P(("dp", "expert"), None),
            P(("dp", "expert"), None),
            P(("dp", "expert"), None),
            P(),
            P(),
            P(),
            P(),
            P("expert", "dp", None),
            P("expert", "dp", None),
        ),
        check_vma=False,
    )
```

profile of v0, /device:TPU:0, one launch (start us, length us, event | category | flops | bytes accessed | tf_op | source)
XLA Modules:
  0.0 455.3 jit_solution(7450179915979604885)
XLA Ops:
  7.2 0.7 all-gather.4.cloned.1.call-update
  8.0 0.7 all-gather.6.cloned.1.call-update
  8.7 0.7 all-gather.8.cloned.1.call-update
  9.4 1.0 fusion.39
  10.5 0.7 fusion.68
  11.2 0.8 broadcast_compare_fusion
  12.3 0.7 select_reduce_fusion
  13.0 0.7 fusion.70
  13.7 102.2 %gather_fusion = s32[16384]{0:T(1024)S(1)} fusion(s32[257]{0:T(512)S(1)} %copy-done.1, s32[16384]{0:T(1024)S(1)} %fusion.52), kind=kCustom, calls=%fused_computation | custom fusion | bytes 196608 | tf_op jit(solution)/shard_map/jit(_take)/gather | solution.py:95
  115.9 0.6 copy-done.22
  116.5 0.7 fusion.22
  117.3 0.4 copy.40
  117.7 3.3 convolution_convert_fusion
  121.9 1.2 fusion.78
  123.5 2.0 multiply_reduce_fusion.3
  126.1 1.0 broadcast_in_dim.76
  127.0 8.3 %all-to-all-start = ((bf16[16,32,768]{2,1,0:T(8,128)(2,1)}), bf16[16,32,768]{2,1,0:T(8,128)(2,1)S(1)}, u32[]{:S(2)}, u32[]{:S(2)}) async-start(bf16[16,32,768]{2,1,0:T(8,128)(2,1)} %bitcast.14), calls=%async_computation | async-start | bytes 1572864 | tf_op jit(solution)/shard_map/all_to_all | solution.py:40
  135.4 19.7 %all-to-all-done = bf16[16,32,768]{2,1,0:T(8,128)(2,1)S(1)} async-done(((bf16[16,32,768]{2,1,0:T(8,128)(2,1)}), bf16[16,32,768]{2,1,0:T(8,128)(2,1)S(1)}, u32[]{:S(2)}, u32[]{:S(2)}) %all-to-all-start) | async-done | bytes 786464 | tf_op jit(solution)/shard_map/all_to_all | solution.py:40
  155.1 5.1 %multiply_convert_fusion = (bf16[512,1536]{1,0:T(8,128)(2,1)S(1)}, f32[512,1536]{1,0:T(8,128)}) fusion(bf16[512,768]{1,0:T(8,128)(2,1)S(1)} %bitcast.100, bf16[1,768,1536]{2,1,0:T(8,128)(2,1)} %all-gather.6.cloned.1.call-done), kind=kOutput, calls=%fused_computation.15 | convolution fusion | flops 1215037440 | bytes 7864320 | tf_op jit(solution)/shard_map/dot_general | solution.py:126
  160.2 4.8 %fusion.13 = f32[16,32,768]{2,1,0:T(8,128)} fusion(bf16[16,32,1536]{2,1,0:T(8,128)(2,1)S(1)} %bitcast.111, bf16[1,768,1536]{2,1,0:T(8,128)(2,1)} %all-gather.8.cloned.1.call-done), kind=kOutput, calls=%fused_computation.21 | convolution fusion | flops 1207959552 | bytes 5505024 | tf_op jit(solution)/shard_map/dot_general | solution.py:27
  165.0 5.0 %all-to-all-start.1 = ((f32[16,32,768]{2,1,0:T(8,128)}), f32[16,32,768]{2,1,0:T(8,128)S(1)}, u32[]{:S(2)}, u32[]{:S(2)}) async-start(f32[16,32,768]{2,1,0:T(8,128)} %fusion.13), calls=%async_computation.1 | async-start | bytes 3145728 | tf_op jit(solution)/shard_map/all_to_all | solution.py:50
  170.3 33.0 %all-to-all-done.1 = f32[16,32,768]{2,1,0:T(8,128)S(1)} async-done(((f32[16,32,768]{2,1,0:T(8,128)}), f32[16,32,768]{2,1,0:T(8,128)S(1)}, u32[]{:S(2)}, u32[]{:S(2)}) %all-to-all-start.1) | async-done | bytes 1572896 | tf_op jit(solution)/shard_map/all_to_all | solution.py:50
  203.4 1.2 fusion.37
  204.6 0.4 convolution_convert_fusion.1
  205.1 27.6 %all_to_all.36 = bf16[16,32,768]{2,1,0:T(8,128)(2,1)S(1)} all-to-all(bf16[16,32,768]{2,1,0:T(8,128)(2,1)S(1)} %bitcast.104), channel_id=1, replica_groups=mesh['dp'=2,'expert'=16] {'expert'}, dimensions={0} | all-to-all | bytes 1572864 | tf_op jit(solution)/shard_map/all_to_all | solution.py:40
  232.7 3.6 convolution_bitcast_fusion
  236.6 5.0 %fusion.7 = bf16[512,1536]{1,0:T(8,128)(2,1)S(1)} fusion(f32[512,1536]{1,0:T(8,128)} %get-tuple-element.31, bf16[512,768]{1,0:T(8,128)(2,1)S(1)} %bitcast.103, bf16[1,768,1536]{2,1,0:T(8,128)(2,1)} %all-gather.8.cloned.1.call-done), kind=kOutput, calls=%fused_computation.14 | convolution fusion | flops 1223688192 | bytes 7864320 | tf_op jit(solution)/shard_map/dot_general | solution.py:139
  241.6 1.2 copy-done.16
  242.7 3.7 convolution_bitcast_fusion.1
  246.4 1.4 copy-done.17
  247.8 4.2 fusion.11
  252.1 4.1 all-to-all-start.3
  256.2 33.5 %all-to-all-done.3 = f32[16,32,768]{2,1,0:T(8,128)S(1)} async-done(((f32[16,32,768]{2,1,0:T(8,128)}), f32[16,32,768]{2,1,0:T(8,128)S(1)}, u32[]{:S(2)}, u32[]{:S(2)}) %all-to-all-start.3) | async-done | bytes 1572896 | tf_op jit(solution)/shard_map/all_to_all | solution.py:50
  289.8 0.4 fusion.46
  290.3 0.9 multiply_reduce_fusion.1
  291.2 1.9 convert_add_fusion
  293.1 1.7 convolution_convert_fusion.6
  295.0 2.5 convolution_convert_fusion.3
  299.1 0.5 fusion.48
  299.8 4.0 fusion.41
  303.8 7.3 %pad_maximum_fusion = f32[3072,768]{1,0:T(8,128)} fusion(f32[768,768]{1,0:T(8,128)S(1)} %fusion.48, f32[2304,768]{1,0:T(8,128)} %fusion.41), kind=kLoop, calls=%fused_computation.2 | loop fusion | flops 2359296 | bytes 18874368 | tf_op jit(solution)/shard_map/concatenate | solution.py:187
  311.1 0.9 copy-done.5
  312.2 0.5 copy.48
  312.7 1.2 fusion.27
  314.0 2.8 fusion.35
  316.8 43.9 %all-reduce = (f32[32,12]{0,1:T(8,128)}, f32[768]{0:T(1024)}, f32[768]{0:T(1024)}, f32[768,8]{0,1:T(8,128)}) all-reduce(f32[32,12]{0,1:T(8,128)S(1)} %fusion.27, f32[768]{0:T(1024)S(1)} %get-tuple-element.11, f32[768]{0:T(1024)S(1)} %copy-done.38, f32[768,8]{0,1:T(8,128)S(1)} %fusion.80), channel_id=1, replica_groups=mesh['dp'=2,'expert'=16] {'dp','expert'}, use_global_device_ids=true, to_apply=%region_17.18 | all-reduce | flops 8064 | bytes 64512 | tf_op jit(solution)/shard_map/psum | solution.py:192
  360.7 0.9 fusion.38
  361.6 86.8 %reduce-scatter.4.cloned.1.call-done = f32[96,768]{1,0:T(8,128)} async-done(((f32[3072,768]{1,0:T(8,128)}), f32[96,768]{1,0:T(8,128)}) %reduce-scatter.4.cloned.1.call-update) | async-done | bytes 294928 | tf_op jit(solution)/shard_map/reduce_scatter | solution.py:186
  (153 shorter events, 5.2 us)
Async XLA Ops:
  7.2 162.9 %copy-start = (bf16[768,8]{0,1:T(8,128)(2,1)S(1)}, bf16[768,8]{0,1:T(8,128)(2,1)}, u32[]{:S(2)}) copy-start(bf16[768,8]{0,1:T(8,128)(2,1)} %param.21) | copy-start | bytes 36868
  7.2 6.5 %copy-start.1 = (s32[257]{0:T(512)S(1)}, s32[257]{0:T(512)}, u32[]{:S(2)}) copy-start(s32[257]{0:T(512)} %param.16) | copy-start | bytes 3088
  7.2 110.5 %all-gather.4.cloned.1.call-start = ((), (), s32[]{:S(2)}) async-start(), calls=%async_computation.7 | async-start | bytes 4866048 | tf_op jit(solution)/shard_map/all_gather | solution.py:80
  7.9 127.4 %all-gather.6.cloned.1.call-start = ((), (), s32[]{:S(2)}) async-start(), calls=%async_computation.8 | async-start | bytes 3538944 | tf_op jit(solution)/shard_map/all_gather | solution.py:82
  8.7 151.5 %all-gather.8.cloned.1.call-start = ((), (), s32[]{:S(2)}) async-start(), calls=%async_computation.9 | async-start | bytes 3538944 | tf_op jit(solution)/shard_map/all_gather | solution.py:83
  10.5 107.2 %copy-start.51 = (f32[128]{0:T(128)}, f32[128]{0:T(128)S(1)}, u32[]{:S(2)}) copy-start(f32[128]{0:T(128)S(1)} %fusion.71) | copy-start | bytes 1540
  13.7 102.9 %copy-start.47 = (f32[32,12]{0,1:T(8,128)S(1)}, f32[32,12]{0,1:T(8,128)}, u32[]{:S(2)}) copy-start(f32[32,12]{0,1:T(8,128)} %param.18) | copy-start | bytes 4612
  13.7 104.0 %copy-start.7 = (bf16[128,768]{1,0:T(8,128)(2,1)S(1)}, bf16[128,768]{1,0:T(8,128)(2,1)}, u32[]{:S(2)}) copy-start(bf16[128,768]{1,0:T(8,128)(2,1)} %param.12) | copy-start | bytes 589828
  13.7 104.0 %copy-start.35 = (f32[768]{0:T(1024)S(1)}, f32[768]{0:T(1024)}, u32[]{:S(2)}) copy-start(f32[768]{0:T(1024)} %param.19) | copy-start | bytes 9220
  121.2 2.2 copy-start.10
  121.4 2.1 copy-start.12
  121.6 1.9 copy-start.26
  121.9 3.6 copy-start.3
  123.2 2.9 copy-start.32
  123.2 2.4 copy-start.30
  123.5 31.6 %copy-start.24 = (bf16[12,64,128]{2,1,0:T(8,128)(2,1)}, bf16[12,64,128]{2,1,0:T(8,128)(2,1)S(1)}, u32[]{:S(2)}) copy-start(bf16[12,64,128]{2,1,0:T(8,128)(2,1)S(1)} %convolution_convert_fusion.7) | copy-start | bytes 589828
  125.5 164.7 %copy-start.48 = (f32[128]{0:T(128)}, f32[128]{0:T(128)S(1)}, u32[]{:S(2)}) copy-start(f32[128]{0:T(128)S(1)} %fusion.72) | copy-start | bytes 1540
  125.7 44.4 %copy-start.4 = (bf16[128,768]{1,0:T(8,128)(2,1)}, bf16[128,768]{1,0:T(8,128)(2,1)S(1)}, u32[]{:S(2)}) copy-start(bf16[128,768]{1,0:T(8,128)(2,1)S(1)} %multiply_convert_fusion.2) | copy-start | bytes 589828
  127.0 28.1 %all-to-all-start = ((bf16[16,32,768]{2,1,0:T(8,128)(2,1)}), bf16[16,32,768]{2,1,0:T(8,128)(2,1)S(1)}, u32[]{:S(2)}, u32[]{:S(2)}) async-start(bf16[16,32,768]{2,1,0:T(8,128)(2,1)} %bitcast.14), calls=%async_computation | async-start | bytes 1572864 | tf_op jit(solution)/shard_map/all_to_all | solution.py:40
  160.2 4.8 %copy-start.14 = (bf16[512,1536]{1,0:T(8,128)(2,1)}, bf16[512,1536]{1,0:T(8,128)(2,1)S(1)}, u32[]{:S(2)}) copy-start(bf16[512,1536]{1,0:T(8,128)(2,1)S(1)} %get-tuple-element.30) | copy-start | bytes 4718596
  165.0 38.4 %copy-start.6 = (bf16[128,768]{1,0:T(8,128)(2,1)S(1)}, bf16[128,768]{1,0:T(8,128)(2,1)}, u32[]{:S(2)}) copy-start(bf16[128,768]{1,0:T(8,128)(2,1)} %param.13) | copy-start | bytes 589828
  165.0 39.6 %copy-start.41 = (s32[128,1]{0,1:T(1,128)S(1)}, s32[128,1]{0,1:T(1,128)}, u32[]{:S(2)}) copy-start(s32[128,1]{0,1:T(1,128)} %param.15) | copy-start | bytes 1540
  165.0 38.3 %all-to-all-start.1 = ((f32[16,32,768]{2,1,0:T(8,128)}), f32[16,32,768]{2,1,0:T(8,128)S(1)}, u32[]{:S(2)}, u32[]{:S(2)}) async-start(f32[16,32,768]{2,1,0:T(8,128)} %fusion.13), calls=%async_computation.1 | async-start | bytes 3145728 | tf_op jit(solution)/shard_map/all_to_all | solution.py:50
  170.0 191.6 %reduce-scatter.8.cloned.1.call-start = ((), (), s32[]{:S(2)}) async-start(), calls=%async_computation.12 | async-start | bytes 7077888 | tf_op jit(solution)/shard_map/reduce_scatter | solution.py:147
  170.2 120.0 %copy-start.39 = (f32[128]{0:T(128)}, f32[128]{0:T(128)S(1)}, u32[]{:S(2)}) copy-start(f32[128]{0:T(128)S(1)} %get-tuple-element.28) | copy-start | bytes 1540
  170.3 119.9 %copy-start.45 = (f32[128]{0:T(128)}, f32[128]{0:T(128)S(1)}, u32[]{:S(2)}) copy-start(f32[128]{0:T(128)S(1)} %fusion.69) | copy-start | bytes 1540
  203.3 29.4 %copy-start.15 = (bf16[512,1536]{1,0:T(8,128)(2,1)S(1)}, bf16[512,1536]{1,0:T(8,128)(2,1)}, u32[]{:S(2)}) copy-start(bf16[512,1536]{1,0:T(8,128)(2,1)} %copy-done.14) | copy-start | bytes 4718596
  204.6 85.7 %copy-start.43 = (f32[128]{0:T(128)}, f32[128]{0:T(128)S(1)}, u32[]{:S(2)}) copy-start(f32[128]{0:T(128)S(1)} %get-tuple-element.32) | copy-start | bytes 1540
  236.4 125.2 %reduce-scatter.6.cloned.1.call-start = ((), (), s32[]{:S(2)}) async-start(), calls=%async_computation.11 | async-start | bytes 7077888 | tf_op jit(solution)/shard_map/reduce_scatter | solution.py:146
  246.4 1.4 copy-start.17
  252.1 37.6 %all-to-all-start.3 = ((f32[16,32,768]{2,1,0:T(8,128)}), f32[16,32,768]{2,1,0:T(8,128)S(1)}, u32[]{:S(2)}, u32[]{:S(2)}) async-start(f32[16,32,768]{2,1,0:T(8,128)} %fusion.11), calls=%async_computation.3 | async-start | bytes 3145728 | tf_op jit(solution)/shard_map/all_to_all | solution.py:50
  256.1 35.1 %copy-start.31 = (f32[768]{0:T(1024)S(1)}, f32[768]{0:T(1024)}, u32[]{:S(2)}) copy-start(f32[768]{0:T(1024)} %param.20) | copy-start | bytes 9220
  256.2 192.3 %reduce-scatter.4.cloned.1.call-start = ((), (), s32[]{:S(2)}) async-start(), calls=%async_computation.10 | async-start | bytes 9732096 | tf_op jit(solution)/shard_map/reduce_scatter | solution.py:186
  256.2 35.0 %copy-start.49 = (f32[128]{0:T(128)}, f32[128]{0:T(128)S(1)}, u32[]{:S(2)}) copy-start(f32[128]{0:T(128)S(1)} %neg.6) | copy-start | bytes 1540
  289.8 5.2 %copy-start.33 = (f32[12,128]{1,0:T(8,128)S(1)}, f32[12,128]{1,0:T(8,128)}, u32[]{:S(2)}) copy-start(f32[12,128]{1,0:T(8,128)} %copy-done.32) | copy-start | bytes 18436
  293.1 4.4 copy-start.2
  293.1 4.4 copy-start.27
  298.5 1.3 copy-start.36
  298.5 1.3 copy-start.52
  311.1 1.7 copy-start.23
  312.0 1.9 copy-start.9
  312.0 1.9 copy-start.19
  312.0 1.9 copy-start.21
  312.0 1.9 copy-start.29
  312.0 1.9 copy-start.37
  312.0 1.9 copy-start.53
  314.0 2.8 copy-start.38
  314.0 46.7 %copy-start.55 = (f32[128]{0:T(128)S(1)}, f32[128]{0:T(128)}, u32[]{:S(2)}) copy-start(f32[128]{0:T(128)} %copy-done.54) | copy-start | bytes 1540
  (17 other events, 16.3 us)
Sparse Core Ops, SparseCore 0:
  10.9 66.3 all-gather.3
  78.8 9.7 all-gather.5
  90.2 12.1 all-gather.7
  236.5 10.3 reduce-scatter.7
  249.7 13.7 reduce-scatter.5
  311.2 137.1 reduce-scatter.3
where the time goes:
time: 456 us; the launch traced here: 455 us
  waiting for transfers between devices  175 us (38%)
  local copies, waits for them, and re-layouts  110 us (24%)
  blocking collectives  71.5 us (16%)
  matrix products  50.2 us (11%)
  starting transfers between devices  17.8 us (4%)
  other arithmetic  15.8 us (3%)
  between operations  14.9 us (3%)
    gather x1, local copies, waits for them, and re-layouts, shards(): bucket = jnp.take(bucket_table, jnp.clip(spacing, -reach, reach) + reach)  102 us
    reduce_scatter x1, waiting for transfers between devices, shards(): lax.psum_scatter(jnp.concatenate([in_block_grad, out_block_grad], axis=0)...  86.8 us
    all_to_all x2, waiting for transfers between devices, collect(): lax.all_to_all(results, 'expert', split_axis=0, concat_axis=0, tiled=True)  66.4 us
    psum x1, blocking collectives, shards(): lax.psum((bias_local, gain_attn_local, gain_ffn_local, router_local), ('d...  43.9 us
    all_to_all x1, blocking collectives, deliver(): lax.all_to_all(doubled.reshape(2 * experts * capacity, width), 'expert',...  27.6 us
    all_to_all x1, waiting for transfers between devices, deliver(): lax.all_to_all(doubled.reshape(2 * experts * capacity, width), 'expert',...  19.7 us
    dot_general x5, matrix products, contract_last(): lax.dot_general(left, right, (((1,), (1,)), ((), ())), preferred_element_...  15.2 us
    dot_general x7, matrix products, contract_first(): lax.dot_general(left, right, (((0,), (0,)), ((), ())), preferred_element_...  12.6 us
  transfers between devices with their start and end apart: 9, of which 4 were waited for; matrix products, arithmetic and copies ran while one was open for 35% of the time, Pallas kernels for 0%

commit v1 on v0

--- a/solution.py
+++ b/solution.py
@@ -29,8 +29,14 @@
     )
 
 
-def select_rows(place, values):
-    return jnp.dot(place, values, precision=lax.Precision.HIGHEST)
+def skewed_table(table, count, reach):
+    offsets = jnp.arange(2 * count)
+    offsets = jnp.where(offsets < count, offsets, offsets - 2 * count)
+    index = jnp.clip(offsets, -reach, reach) + reach
+    hot = index[:, None] == jnp.arange(table.shape[0])[None, :]
+    line = jnp.sum(jnp.where(hot, table[None, :], 0), axis=1)
+    flat = jnp.broadcast_to(line[None, :], (count, 2 * count)).reshape(-1)
+    return flat[: count * (2 * count - 1)].reshape(count, 2 * count - 1)[:, :count]
 
 
 def deliver(buffer, experts, capacity, width):
@@ -48,9 +54,8 @@
 
 def collect(results, experts, capacity, width):
     returned = lax.all_to_all(results, "expert", split_axis=0, concat_axis=0, tiled=True)
-    return jnp.sum(returned.reshape(experts, 2, capacity, width), axis=1).reshape(
-        experts * capacity, width
-    )
+    returned = returned.reshape(experts, 2, capacity, width)
+    return [returned[:, half].reshape(experts * capacity, width) for half in (0, 1)]
 
 
 def shards(
@@ -91,8 +96,7 @@
     queries = qkv[:, :width].reshape(count, heads, head_dim)
     keys = qkv[:, width : 2 * width].reshape(count, heads, head_dim)
     values = qkv[:, 2 * width :].reshape(count, heads, head_dim)
-    spacing = jnp.arange(count)[None, :] - jnp.arange(count)[:, None]
-    bucket = jnp.take(bucket_table, jnp.clip(spacing, -reach, reach) + reach)
+    bucket = skewed_table(bucket_table, count, reach)
     bucket_hot = (bucket[:, :, None] == jnp.arange(buckets)[None, None, :]).astype(f32)
     bias = jnp.einsum("ijb,bh->hij", bucket_hot, rel_bias, precision=highest)
     segment = segment_ids[0]
@@ -115,40 +119,43 @@
     route = routes[:, 0]
     chosen = (route[:, None] == jnp.arange(experts)[None, :]).astype(f32)
     gate, gate_back = jax.vjp(lambda scores_in: gate_value(scores_in, chosen), logits)
-    earlier = jnp.cumsum(chosen, axis=0) - chosen
+    below = (jnp.arange(count)[:, None] > jnp.arange(count)[None, :]).astype(bf16)
+    earlier = jnp.dot(below, chosen.astype(bf16), preferred_element_type=f32)
     slot = jnp.sum(earlier * chosen, axis=1).astype(jnp.int32)
     column = route * capacity + slot
     place_hot = column[:, None] == jnp.arange(experts * capacity)[None, :]
     place = place_hot.astype(bf16)
-    place_wide = place_hot.astype(f32)
-    buffer = contract_first(place, normed_two).astype(bf16)
-    arrived = deliver(buffer, experts, capacity, width)
+    upstream = cotangent.astype(f32)
+    expert_grad_tok = (gate[:, None] * upstream).astype(bf16)
+    both = jnp.concatenate([normed_two, expert_grad_tok], axis=1)
+    buffer = contract_first(place, both).astype(bf16)
+    arrived_both = deliver(buffer, experts, capacity, 2 * width)
+    arrived, grad_arrived = arrived_both[:, :width], arrived_both[:, width:]
     hidden = jnp.dot(arrived, w_inner, preferred_element_type=f32)
     active, active_back = jax.vjp(tanh_gelu, hidden)
     active_low = active.astype(bf16)
-    partial_rows = contract_last(active_low, w_outer)
-    expert_rows = collect(partial_rows, experts, capacity, width)
-    expert_tok = select_rows(place_wide, expert_rows)
-    mixed = (x_mid + gate[:, None] * expert_tok).astype(bf16)
-    upstream = cotangent.astype(f32)
-    gate_grad = jnp.sum(upstream * expert_tok, axis=1)
-    expert_grad_tok = (gate[:, None] * upstream).astype(bf16)
-    grad_arrived = deliver(
-        contract_first(place, expert_grad_tok).astype(bf16), experts, capacity, width
-    )
+    partial_rows = contract_last(active_low, w_outer).astype(bf16)
     active_grad = jnp.dot(grad_arrived, w_outer, preferred_element_type=f32)
     hidden_grad = active_back(active_grad)[0].astype(bf16)
-    input_part = contract_last(hidden_grad, w_inner)
-    input_rows = collect(input_part, experts, capacity, width)
+    input_part = contract_last(hidden_grad, w_inner).astype(bf16)
     outer_grad = contract_first(grad_arrived, active_low)
     inner_grad = contract_first(arrived, hidden_grad)
     inner_share, outer_share = (
         lax.psum_scatter(inner_grad[None], "dp", scatter_dimension=1, tiled=True),
         lax.psum_scatter(outer_grad[None], "dp", scatter_dimension=1, tiled=True),
     )
+    results = collect(
+        jnp.concatenate([partial_rows, input_part], axis=1), experts, capacity, 2 * width
+    )
+    tok_both = jnp.dot(place, results[0], preferred_element_type=f32) + jnp.dot(
+        place, results[1], preferred_element_type=f32
+    )
+    expert_tok, input_tok = tok_both[:, :width], tok_both[:, width:]
+    mixed = (x_mid + gate[:, None] * expert_tok).astype(bf16)
+    gate_grad = jnp.sum(upstream * expert_tok, axis=1)
     logit_grad = gate_back(gate_grad)[0].astype(bf16)
     router_local = contract_first(normed_two, logit_grad)
-    norm_two_grad = select_rows(place_wide, input_rows) + contract_last(logit_grad, router_weight)
+    norm_two_grad = input_tok + contract_last(logit_grad, router_weight)
     mid_part, gain_ffn_local = norm_two_back(norm_two_grad)
     mid_grad = upstream + mid_part
     branch_grad = mid_grad.astype(bf16)
@@ -184,14 +191,19 @@
     input_part_one, gain_attn_local = norm_one_back(norm_one_grad)
     tokens_grad = mid_grad + input_part_one
     mixer_grad = lax.psum_scatter(
-        jnp.concatenate([in_block_grad, out_block_grad], axis=0),
+        jnp.concatenate([in_block_grad, out_block_grad], axis=0).astype(bf16),
         ("dp", "expert"),
         scatter_dimension=0,
         tiled=True,
-    )
-    bias_sum, attn_gain_sum, ffn_gain_sum, router_sum = lax.psum(
-        (bias_local, gain_attn_local, gain_ffn_local, router_local), ("dp", "expert")
-    )
+    ).astype(f32)
+    pieces = (bias_local, gain_attn_local, gain_ffn_local, router_local)
+    flat = jnp.concatenate([piece.reshape(-1) for piece in pieces])
+    total = lax.psum(flat.reshape(-1, 128), ("dp", "expert")).reshape(-1)
+    sums, start = [], 0
+    for piece in pieces:
+        sums.append(total[start : start + piece.size].reshape(piece.shape))
+        start += piece.size
+    bias_sum, attn_gain_sum, ffn_gain_sum, router_sum = sums
     return (
         mixed,
         tokens_grad,

time: 456 us -> 348 us (0.76)
  local copies, waits for them, and re-layouts: 110 us -> 9.6 us
  waiting for transfers between devices: 175 us -> 207 us
  blocking collectives: 71.5 us -> 43.1 us
  starting transfers between devices: 17.8 us -> 12.9 us
    gather x1 -> x0, local copies, waits for them, and re-layouts: 102 us -> none  [shards(): bucket = jnp.take(bucket_table, jnp.clip(spacing, -reach, reach) + reach)]
    all_gather x1, waiting for transfers between devices: 0.02 us -> 63 us  [shards(): mixer = lax.all_gather(mixer_weight, ('dp', 'expert'), axis=0, tiled=True)]
    reduce_scatter x1, waiting for transfers between devices: 86.8 us -> 46.4 us  [shards(): lax.psum_scatter(jnp.concatenate([in_block_grad, out_block_grad], axis=0)...]
    all_to_all x2 -> x1, waiting for transfers between devices: 66.4 us -> 32.3 us  [collect(): lax.all_to_all(results, 'expert', split_axis=0, concat_axis=0, tiled=True)]
    all_to_all x1 -> x0, blocking collectives: 27.6 us -> none  [deliver(): lax.all_to_all(doubled.reshape(2 * experts * capacity, width), 'expert',...]
    reduce_scatter x1, waiting for transfers between devices: 0.01 us -> 16.5 us  [shards(): lax.psum_scatter(outer_grad[None], 'dp', scatter_dimension=1, tiled=True)]
    all_to_all x1, waiting for transfers between devices: 19.7 us -> 33.5 us  [deliver(): lax.all_to_all(doubled.reshape(2 * experts * capacity, width), 'expert',...]
    reduce_scatter x1, waiting for transfers between devices: 0.01 us -> 13 us  [shards(): lax.psum_scatter(inner_grad[None], 'dp', scatter_dimension=1, tiled=True)]
  transfers between devices with their start and end apart: 9 -> 8, of which waited for: 4 -> 6; matrix products, arithmetic and copies ran while one was open for 35% -> 12% of each run, Pallas kernels for 0% -> 0%
where the time goes in v1:
time: 348 us; the launch traced here: 347 us
  waiting for transfers between devices  207 us (59%)
  matrix products  47 us (14%)
  blocking collectives  43.1 us (12%)
  between operations  15.1 us (4%)
  starting transfers between devices  12.9 us (4%)
  other arithmetic  12.7 us (4%)
  local copies, waits for them, and re-layouts  9.6 us (3%)
    all_gather x1, waiting for transfers between devices, shards(): mixer = lax.all_gather(mixer_weight, ('dp', 'expert'), axis=0, tiled=True)  63 us
    reduce_scatter x1, waiting for transfers between devices, shards(): lax.psum_scatter(jnp.concatenate([in_block_grad, out_block_grad], axis=0)...  46.4 us
    psum x1, blocking collectives, shards(): total = lax.psum(flat.reshape(-1, 128), ('dp', 'expert')).reshape(-1)  43.1 us
    all_to_all x1, waiting for transfers between devices, deliver(): lax.all_to_all(doubled.reshape(2 * experts * capacity, width), 'expert',...  33.5 us
    all_to_all x1, waiting for transfers between devices, collect(): lax.all_to_all(results, 'expert', split_axis=0, concat_axis=0, tiled=True)  32.3 us
    reduce_scatter x1, waiting for transfers between devices, shards(): lax.psum_scatter(outer_grad[None], 'dp', scatter_dimension=1, tiled=True)  16.5 us
    dot_general x6, matrix products, contract_first(): lax.dot_general(left, right, (((0,), (0,)), ((), ())), preferred_element_...  13.9 us
    reduce_scatter x1, waiting for transfers between devices, shards(): lax.psum_scatter(inner_grad[None], 'dp', scatter_dimension=1, tiled=True)  13 us
  transfers between devices with their start and end apart: 8, of which 6 were waited for; matrix products, arithmetic and copies ran while one was open for 12% of the time, Pallas kernels for 0%

profile of v1, /device:TPU:0, one launch (start us, length us, event | category | flops | bytes accessed | tf_op | source)
XLA Modules:
  0.0 347.3 jit_solution(7198675047271176321)
XLA Ops:
  7.3 0.7 all-gather.4.cloned.1.call-update
  8.0 0.7 all-gather.6.cloned.1.call-update
  8.7 1.0 fusion.50
  9.8 0.5 copy-done.54
  10.3 0.8 select_reduce_fusion
  11.5 0.6 copy-done.19
  12.1 1.4 fusion.22
  14.2 63.0 %all-gather.4.cloned.1.call-done = bf16[3072,768]{1,0:T(8,128)(2,1)} async-done(((bf16[96,768]{1,0:T(8,128)(2,1)}), bf16[3072,768]{1,0:T(8,128)(2,1)}) %all-gather.4.cloned.1.call-update) | async-done | bytes 4718608 | tf_op jit(solution)/shard_map/all_gather | solution.py:85
  77.3 3.3 convolution_convert_fusion.1
  81.3 1.1 fusion.85
  83.1 2.1 multiply_reduce_fusion.3
  85.2 0.6 copy-done.59
  86.1 0.5 copy-done.29
  87.3 1.3 broadcast_in_dim.50
  88.6 4.4 %all-to-all-start = ((bf16[16,32,1536]{2,1,0:T(8,128)(2,1)}), bf16[16,32,1536]{2,1,0:T(8,128)(2,1)S(1)}, u32[]{:S(2)}, u32[]{:S(2)}) async-start(bf16[16,32,1536]{2,1,0:T(8,128)(2,1)} %bitcast.12), calls=%async_computation | async-start | bytes 3145728 | tf_op jit(solution)/shard_map/all_to_all | solution.py:46
  93.1 0.7 all-gather.8.cloned.1.call-update
  93.8 33.5 %all-to-all-done = bf16[16,32,1536]{2,1,0:T(8,128)(2,1)S(1)} async-done(((bf16[16,32,1536]{2,1,0:T(8,128)(2,1)}), bf16[16,32,1536]{2,1,0:T(8,128)(2,1)S(1)}, u32[]{:S(2)}, u32[]{:S(2)}) %all-to-all-start) | async-done | bytes 1572896 | tf_op jit(solution)/shard_map/all_to_all | solution.py:46
  127.3 4.8 %fusion.19 = f32[512,1536]{1,0:T(8,128)} fusion(bf16[1,768,1536]{2,1,0:T(8,128)(2,1)} %all-gather.6.cloned.1.call-done, bf16[512,1536]{1,0:T(8,128)(2,1)S(1)} %bitcast.91), kind=kOutput, calls=%fused_computation.27 | convolution fusion | flops 1207959552 | bytes 6291456 | tf_op jit(solution)/shard_map/dot_general | solution.py:134
  132.0 5.1 %fusion.7 = bf16[512,1536]{1,0:T(8,128)(2,1)S(1)} fusion(f32[512,1536]{1,0:T(8,128)} %fusion.19, bf16[1,768,1536]{2,1,0:T(8,128)(2,1)} %all-gather.8.cloned.1.call-done, bf16[512,1536]{1,0:T(8,128)(2,1)S(1)} %bitcast.92), kind=kOutput, calls=%fused_computation.14 | convolution fusion | flops 1223688192 | bytes 7864320 | tf_op jit(solution)/shard_map/dot_general | solution.py:138
  137.2 2.0 fusion.27
  139.4 1.4 fusion.24
  140.8 1.3 pad_maximum_fusion.1
  142.1 8.1 %all-to-all-start.1 = ((bf16[16,32,1536]{2,1,0:T(8,128)(2,1)}), bf16[16,32,1536]{2,1,0:T(8,128)(2,1)S(1)}, u32[]{:S(2)}, u32[]{:S(2)}) async-start(bf16[16,32,1536]{2,1,0:T(8,128)(2,1)} %bitcast.16), calls=%async_computation.1 | async-start | bytes 3145728 | tf_op jit(solution)/shard_map/all_to_all | solution.py:56
  150.4 1.2 multiply_divide_fusion
  151.6 32.3 %all-to-all-done.1 = bf16[16,32,1536]{2,1,0:T(8,128)(2,1)S(1)} async-done(((bf16[16,32,1536]{2,1,0:T(8,128)(2,1)}), bf16[16,32,1536]{2,1,0:T(8,128)(2,1)S(1)}, u32[]{:S(2)}, u32[]{:S(2)}) %all-to-all-start.1) | async-done | bytes 1572896 | tf_op jit(solution)/shard_map/all_to_all | solution.py:56
  185.2 0.8 fusion.48
  186.1 0.9 multiply_reduce_fusion.1
  187.2 1.7 convolution_convert_fusion.7
  189.1 1.6 multiply_reduce_fusion
  190.7 0.8 subtract_multiply_fusion
  192.3 2.6 convolution_convert_fusion.4
  194.9 0.5 convolution_convert_fusion.3
  195.4 2.1 convolution_convert_fusion
  197.5 2.5 pad_maximum_fusion
  200.0 5.1 %convolution_bitcast_fusion.1 = f32[1,768,1536]{2,1,0:T(8,128)} fusion(bf16[512,1536]{1,0:T(8,128)(2,1)} %copy-done.14, bf16[512,1536]{1,0:T(8,128)(2,1)S(1)} %bitcast.93), kind=kOutput, calls=%fused_computation.6 | convolution fusion | flops 1207959552 | bytes 7077888 | tf_op jit(solution)/shard_map/dot_general | solution.py:21
  205.2 5.6 %convolution_bitcast_fusion = f32[1,768,1536]{2,1,0:T(8,128)} fusion(bf16[512,1536]{1,0:T(8,128)(2,1)S(1)} %bitcast.94, f32[512,1536]{1,0:T(8,128)} %fusion.19), kind=kOutput, calls=%fused_computation.5 | convolution fusion | flops 1215037440 | bytes 8650752 | tf_op jit(solution)/shard_map/dot_general | solution.py:21
  210.9 0.5 copy.58
  212.2 1.2 fusion.33
  213.5 2.9 fusion.46
  216.5 43.1 %psum.7 = f32[63,128]{1,0:T(8,128)S(1)} all-reduce(f32[63,128]{1,0:T(8,128)S(1)} %maximum_bitcast_fusion), channel_id=1, replica_groups=mesh['dp'=2,'expert'=16] {'dp','expert'}, use_global_device_ids=true, to_apply=%region_17.18 | all-reduce | flops 8064 | bytes 64512 | tf_op jit(solution)/shard_map/psum | solution.py:201
  259.8 0.7 copy.62
  260.6 0.7 copy.61
  261.3 0.6 slice_bitcast_fusion
  261.9 0.9 fusion.49
  262.8 46.4 %reduce-scatter.4.cloned.1.call-done = bf16[96,768]{1,0:T(8,128)(2,1)} async-done(((bf16[3072,768]{1,0:T(8,128)(2,1)}), bf16[96,768]{1,0:T(8,128)(2,1)}) %reduce-scatter.4.cloned.1.call-update) | async-done | bytes 147472 | tf_op jit(solution)/shard_map/reduce_scatter | solution.py:193
  309.3 1.6 convert_element_type.130
  310.9 13.0 %reduce-scatter.6.cloned.1.call-done = f32[1,384,1536]{2,1,0:T(8,128)} async-done(((f32[1,768,1536]{2,1,0:T(8,128)}), f32[1,384,1536]{2,1,0:T(8,128)}) %reduce-scatter.6.cloned.1.call-update) | async-done | bytes 2359312 | tf_op jit(solution)/shard_map/reduce_scatter | solution.py:144
  323.9 16.5 %reduce-scatter.8.cloned.1.call-done = f32[1,384,1536]{2,1,0:T(8,128)} async-done(((f32[1,768,1536]{2,1,0:T(8,128)}), f32[1,384,1536]{2,1,0:T(8,128)}) %reduce-scatter.8.cloned.1.call-update) | async-done | bytes 2359312 | tf_op jit(solution)/shard_map/reduce_scatter | solution.py:145
  (173 shorter events, 7.6 us)
Async XLA Ops:
  7.2 78.7 %copy-start = (bf16[768,8]{0,1:T(8,128)(2,1)S(1)}, bf16[768,8]{0,1:T(8,128)(2,1)}, u32[]{:S(2)}) copy-start(bf16[768,8]{0,1:T(8,128)(2,1)} %param.21) | copy-start | bytes 36868
  7.2 70.1 %copy-start.7 = (bf16[128,768]{1,0:T(8,128)(2,1)S(1)}, bf16[128,768]{1,0:T(8,128)(2,1)}, u32[]{:S(2)}) copy-start(bf16[128,768]{1,0:T(8,128)(2,1)} %param.12) | copy-start | bytes 589828
  7.2 6.7 %copy-start.51 = (s32[1,128]{1,0:T(1,128)S(1)}, s32[1,128]{1,0:T(1,128)}, u32[]{:S(2)}) copy-start(s32[1,128]{1,0:T(1,128)} %param.14) | copy-start | bytes 1540
  7.2 6.8 %copy-start.40 = (s32[128,1]{0,1:T(1,128)S(1)}, s32[128,1]{0,1:T(1,128)}, u32[]{:S(2)}) copy-start(s32[128,1]{0,1:T(1,128)} %param.15) | copy-start | bytes 1540
  7.2 70.0 %copy-start.33 = (f32[768]{0:T(1024)S(1)}, f32[768]{0:T(1024)}, u32[]{:S(2)}) copy-start(f32[768]{0:T(1024)} %param.19) | copy-start | bytes 9220
  7.2 70.0 %all-gather.4.cloned.1.call-start = ((), (), s32[]{:S(2)}) async-start(), calls=%async_computation.5 | async-start | bytes 4866048 | tf_op jit(solution)/shard_map/all_gather | solution.py:85
  8.0 85.8 %all-gather.6.cloned.1.call-start = ((), (), s32[]{:S(2)}) async-start(), calls=%async_computation.6 | async-start | bytes 3538944 | tf_op jit(solution)/shard_map/all_gather | solution.py:87
  10.3 70.3 %copy-start.52 = (f32[128]{0:T(128)}, f32[128]{0:T(128)S(1)}, u32[]{:S(2)}) copy-start(f32[128]{0:T(128)S(1)} %fusion.76) | copy-start | bytes 1540
  14.2 72.6 %copy-start.45 = (s32[128]{0:T(128)}, s32[128]{0:T(128)S(1)}, u32[]{:S(2)}) copy-start(s32[128]{0:T(128)S(1)} %fusion.75) | copy-start | bytes 1540
  80.8 2.2 copy-start.10
  81.0 2.0 copy-start.12
  81.3 3.8 %copy-start.1 = (f32[12,128,128]{1,2,0:T(8,128)}, f32[12,128,128]{1,2,0:T(8,128)S(1)}, u32[]{:S(2)}) copy-start(f32[12,128,128]{1,2,0:T(8,128)S(1)} %fusion.32) | copy-start | bytes 2359300
  82.5 3.3 copy-start.26
  82.6 49.4 %copy-start.23 = (bf16[128,768]{0,1:T(8,128)(2,1)}, bf16[128,768]{0,1:T(8,128)(2,1)S(1)}, u32[]{:S(2)}) copy-start(bf16[128,768]{0,1:T(8,128)(2,1)S(1)} %copy.49) | copy-start | bytes 589828
  82.6 4.0 %copy-start.5 = (bf16[128,768]{1,0:T(8,128)(2,1)S(1)}, bf16[128,768]{1,0:T(8,128)(2,1)}, u32[]{:S(2)}) copy-start(bf16[128,768]{1,0:T(8,128)(2,1)} %param.13) | copy-start | bytes 589828
  83.1 3.0 copy-start.21
  85.7 2.8 copy-start.43
  85.9 2.7 copy-start.3
  88.6 38.7 %all-to-all-start = ((bf16[16,32,1536]{2,1,0:T(8,128)(2,1)}), bf16[16,32,1536]{2,1,0:T(8,128)(2,1)S(1)}, u32[]{:S(2)}, u32[]{:S(2)}) async-start(bf16[16,32,1536]{2,1,0:T(8,128)(2,1)} %bitcast.12), calls=%async_computation | async-start | bytes 3145728 | tf_op jit(solution)/shard_map/all_to_all | solution.py:46
  93.0 39.0 %all-gather.8.cloned.1.call-start = ((), (), s32[]{:S(2)}) async-start(), calls=%async_computation.7 | async-start | bytes 3538944 | tf_op jit(solution)/shard_map/all_gather | solution.py:88
  132.0 5.1 %copy-start.58 = (bf16[1,768,1536]{2,1,0:T(8,128)(2,1)S(1)}, bf16[1,768,1536]{2,1,0:T(8,128)(2,1)}, u32[]{:S(2)}) copy-start(bf16[1,768,1536]{2,1,0:T(8,128)(2,1)} %all-gather.8.cloned.1.call-done) | copy-start | bytes 7077892
  132.0 5.1 %copy-start.61 = (f32[512,1536]{1,0:T(8,128)S(1)}, f32[512,1536]{1,0:T(8,128)}, u32[]{:S(2)}) copy-start(f32[512,1536]{1,0:T(8,128)} %fusion.19) | copy-start | bytes 9437188
  137.2 3.7 %copy-start.14 = (bf16[512,1536]{1,0:T(8,128)(2,1)}, bf16[512,1536]{1,0:T(8,128)(2,1)S(1)}, u32[]{:S(2)}) copy-start(bf16[512,1536]{1,0:T(8,128)(2,1)S(1)} %fusion.7) | copy-start | bytes 4718596
  137.2 2.2 copy-start.57
  142.1 41.8 %all-to-all-start.1 = ((bf16[16,32,1536]{2,1,0:T(8,128)(2,1)}), bf16[16,32,1536]{2,1,0:T(8,128)(2,1)S(1)}, u32[]{:S(2)}, u32[]{:S(2)}) async-start(bf16[16,32,1536]{2,1,0:T(8,128)(2,1)} %bitcast.16), calls=%async_computation.1 | async-start | bytes 3145728 | tf_op jit(solution)/shard_map/all_to_all | solution.py:56
  150.2 159.1 %reduce-scatter.4.cloned.1.call-start = ((), (), s32[]{:S(2)}) async-start(), calls=%async_computation.8 | async-start | bytes 4866048 | tf_op jit(solution)/shard_map/reduce_scatter | solution.py:193
  184.0 2.0 copy-start.30
  184.1 2.0 copy-start.27
  184.1 2.0 copy-start.38
  184.1 2.0 copy-start.44
  184.5 2.5 copy-start.60
  187.2 3.5 %copy-start.2 = (f32[12,128,128]{1,2,0:T(8,128)S(1)}, f32[12,128,128]{1,2,0:T(8,128)}, u32[]{:S(2)}) copy-start(f32[12,128,128]{1,2,0:T(8,128)} %get-tuple-element.41) | copy-start | bytes 2359300
  189.1 2.5 copy-start.13
  189.1 2.8 copy-start.11
  191.6 3.3 copy-start.22
  191.8 3.5 %copy-start.15 = (bf16[12,64,128]{2,1,0:T(8,128)(2,1)}, bf16[12,64,128]{2,1,0:T(8,128)(2,1)S(1)}, u32[]{:S(2)}) copy-start(bf16[12,64,128]{2,1,0:T(8,128)(2,1)S(1)} %convolution_convert_fusion.6) | copy-start | bytes 589828
  191.9 3.5 %copy-start.8 = (bf16[128,768]{1,0:T(8,128)(2,1)S(1)}, bf16[128,768]{1,0:T(8,128)(2,1)}, u32[]{:S(2)}) copy-start(bf16[128,768]{1,0:T(8,128)(2,1)} %param.12) | copy-start | bytes 589828
  192.2 5.2 %copy-start.17 = (bf16[12,64,128]{2,1,0:T(8,128)(2,1)}, bf16[12,64,128]{2,1,0:T(8,128)(2,1)S(1)}, u32[]{:S(2)}) copy-start(bf16[12,64,128]{2,1,0:T(8,128)(2,1)S(1)} %convolution_convert_fusion.5) | copy-start | bytes 589828
  200.0 123.9 %reduce-scatter.6.cloned.1.call-start = ((), (), s32[]{:S(2)}) async-start(), calls=%async_computation.9 | async-start | bytes 7077888 | tf_op jit(solution)/shard_map/reduce_scatter | solution.py:144
  205.1 135.3 %reduce-scatter.8.cloned.1.call-start = ((), (), s32[]{:S(2)}) async-start(), calls=%async_computation.10 | async-start | bytes 7077888 | tf_op jit(solution)/shard_map/reduce_scatter | solution.py:145
  210.8 2.6 copy-start.9
  210.8 2.6 copy-start.16
  210.8 2.6 copy-start.18
  210.8 2.6 copy-start.25
  210.9 2.6 copy-start.34
  210.9 2.6 copy-start.53
  213.5 2.9 copy-start.32
  213.5 47.8 %copy-start.55 = (f32[128]{0:T(128)S(1)}, f32[128]{0:T(128)}, u32[]{:S(2)}) copy-start(f32[128]{0:T(128)} %copy-done.54) | copy-start | bytes 1540
  (22 other events, 23.1 us)
Sparse Core Ops, SparseCore 0:
  11.0 66.2 all-gather.3
  78.8 9.7 all-gather.5
  95.4 12.2 all-gather.7
  200.1 109.1 reduce-scatter.3
  312.1 11.7 reduce-scatter.5
  326.7 13.7 reduce-scatter.7

commit v2 on v1

--- a/solution.py
+++ b/solution.py
@@ -1,6 +1,8 @@
 import jax
 import jax.numpy as jnp
 from jax import lax
+from jax.experimental import pallas as pl
+from jax.experimental.pallas import tpu as pltpu
 from jax.sharding import PartitionSpec as P
 
 
@@ -56,6 +58,236 @@
     returned = lax.all_to_all(results, "expert", split_axis=0, concat_axis=0, tiled=True)
     returned = returned.reshape(experts, 2, capacity, width)
     return [returned[:, half].reshape(experts * capacity, width) for half in (0, 1)]
+
+
+MESH = pl.DeviceIdType.MESH
+
+
+def coordinates():
+    core, chip = lax.axis_index("dp"), lax.axis_index("expert")
+    bits = [chip // 8, (chip // 4) % 2, (chip // 2) % 2, chip % 2]
+    partners = [(core, chip + (1 - 2 * bit) * step) for bit, step in zip(bits, (8, 4, 2, 1))]
+    return core, bits, (1 - core, chip), partners
+
+
+def meet(partners):
+    barrier = pltpu.get_barrier_semaphore()
+    for partner in partners:
+        pl.semaphore_signal(barrier, inc=1, device_id=partner, device_id_type=MESH)
+    pl.semaphore_wait(barrier, len(partners))
+
+
+def gather_kernel(own_ref, out_ref, local_sem, send_sem, recv_sem):
+    core, (high, low, y, x), sibling, (to_high, to_low, to_y, to_x) = coordinates()
+    half = own_ref.shape[1] // 2
+    left, right = pl.ds(0, half), pl.ds(half, half)
+    every = slice(None)
+    local = pltpu.make_async_copy(own_ref, out_ref.at[core, high, low, y, x], local_sem)
+    local.start()
+    meet((sibling, to_high, to_low, to_y, to_x))
+    local.wait()
+
+    def send(number, where, target):
+        copy = pltpu.make_async_remote_copy(
+            src_ref=out_ref.at[where],
+            dst_ref=out_ref.at[where],
+            send_sem=send_sem.at[number],
+            recv_sem=recv_sem.at[number],
+            device_id=target,
+            device_id_type=MESH,
+        )
+        copy.start()
+        return copy
+
+    first = send(0, (core, high, low, y, x), to_high)
+    first.wait_recv()
+    second = send(1, (core, every, low, y, x), to_low)
+    second.wait_recv()
+    third_a = send(2, (core, every, every, y, x, every, left), to_y)
+    third_b = send(3, (core, every, every, y, x, every, right), to_x)
+    across = [send(6, (core, every, every, y, x), sibling)]
+    third_a.wait_recv()
+    fourth_a = send(4, (core, every, every, every, x, every, left), to_x)
+    third_b.wait_recv()
+    fourth_b = send(5, (core, every, every, y, every, every, right), to_y)
+    across.append(send(7, (core, every, every, 1 - y, x, every, left), sibling))
+    across.append(send(8, (core, every, every, y, 1 - x, every, right), sibling))
+    fourth_a.wait_recv()
+    across.append(send(9, (core, every, every, every, 1 - x, every, left), sibling))
+    fourth_b.wait_recv()
+    across.append(send(10, (core, every, every, 1 - y, every, every, right), sibling))
+    for copy in across:
+        copy.wait_recv()
+    for copy in [first, second, third_a, third_b, fourth_a, fourth_b] + across:
+        copy.wait_send()
+
+
+def gather_mixer(block):
+    rows, width = block.shape
+    out = pl.pallas_call(
+        gather_kernel,
+        out_shape=jax.ShapeDtypeStruct((2, 2, 2, 2, 2, rows, width), block.dtype),
+        in_specs=[pl.BlockSpec(memory_space=pl.ANY)],
+        out_specs=pl.BlockSpec(memory_space=pl.ANY),
+        scratch_shapes=[
+            pltpu.SemaphoreType.DMA,
+            pltpu.SemaphoreType.DMA((11,)),
+            pltpu.SemaphoreType.DMA((11,)),
+        ],
+        compiler_params=pltpu.CompilerParams(collective_id=0, has_side_effects=True),
+    )(block)
+    return out.reshape(32 * rows, width)
+
+
+def scatter_kernel(
+    grad_ref,
+    small_ref,
+    out_ref,
+    total_ref,
+    whole,
+    pair,
+    quad,
+    line,
+    from_core,
+    from_a,
+    from_b,
+    then_a,
+    then_b,
+    from_low,
+    from_high,
+    sums,
+    arrived,
+    send_sem,
+    recv_sem,
+):
+    core, (high, low, y, x), sibling, (to_high, to_low, to_y, to_x) = coordinates()
+    f32, bf16 = jnp.float32, jnp.bfloat16
+    half = out_ref.shape[1] // 2
+    left, right = pl.ds(0, half), pl.ds(half, half)
+    every = slice(None)
+    meet((sibling, to_high, to_low, to_y, to_x))
+
+    def send(number, source, target_ref, target):
+        copy = pltpu.make_async_remote_copy(
+            src_ref=source,
+            dst_ref=target_ref,
+            send_sem=send_sem.at[number],
+            recv_sem=recv_sem.at[number],
+            device_id=target,
+            device_id_type=MESH,
+        )
+        copy.start()
+        return copy
+
+    started = []
+    order = (sibling, to_x, to_y, to_low, to_high)
+
+    def small_start(stage):
+        copy = send(7 + stage, sums.at[stage], arrived.at[stage], order[stage])
+        started.append(copy)
+        return copy
+
+    def small_end(stage, copy):
+        copy.wait_recv()
+        sums[stage + 1] = sums[stage] + arrived[stage]
+
+    def add(one, two):
+        return one.astype(f32) + two.astype(f32)
+
+    sums[0] = small_ref[...]
+    copy = send(0, grad_ref.at[1 - core], from_core, sibling)
+    small = small_start(0)
+    copy.wait_recv()
+    started.append(copy)
+    for a in (0, 1):
+        for b in (0, 1):
+            for c in (0, 1):
+                for d in (0, 1):
+                    whole[a, b, c, d] = add(
+                        grad_ref[core, a, b, c, d], from_core[a, b, c, d]
+                    ).astype(bf16)
+    one = send(1, whole.at[:, :, :, 1 - x, :, left], from_a, to_x)
+    two = send(2, whole.at[:, :, 1 - y, :, :, right], from_b, to_y)
+    started += [one, two]
+    small_end(0, small)
+    small = small_start(1)
+    one.wait_recv()
+    for a in (0, 1):
+        for b in (0, 1):
+            for c in (0, 1):
+                pair[0, a, b, c] = add(whole[a, b, c, x, :, :half], from_a[a, b, c]).astype(bf16)
+    three = send(3, pair.at[0, :, :, 1 - y], then_a, to_y)
+    two.wait_recv()
+    for a in (0, 1):
+        for b in (0, 1):
+            for c in (0, 1):
+                pair[1, a, b, c] = add(whole[a, b, y, c, :, half:], from_b[a, b, c]).astype(bf16)
+    four = send(4, pair.at[1, :, :, 1 - x], then_b, to_x)
+    started += [three, four]
+    small_end(1, small)
+    small = small_start(2)
+    three.wait_recv()
+    four.wait_recv()
+    for a in (0, 1):
+        for b in (0, 1):
+            quad[a, b, :, :half] = add(pair[0, a, b, y], then_a[a, b]).astype(bf16)
+            quad[a, b, :, half:] = add(pair[1, a, b, x], then_b[a, b]).astype(bf16)
+    five = send(5, quad.at[:, 1 - low], from_low, to_low)
+    started.append(five)
+    small_end(2, small)
+    small = small_start(3)
+    five.wait_recv()
+    for a in (0, 1):
+        line[a] = add(quad[a, low], from_low[a]).astype(bf16)
+    six = send(6, line.at[1 - high], from_high, to_high)
+    started.append(six)
+    small_end(3, small)
+    small = small_start(4)
+    six.wait_recv()
+    out_ref[...] = add(line[high], from_high[...])
+    small.wait_recv()
+    total_ref[...] = sums[4] + arrived[4]
+    for copy in started:
+        copy.wait_send()
+
+
+def scatter_mixer(grad, small):
+    rows, width = grad.shape[0] // 32, grad.shape[1]
+    bf16, f32 = grad.dtype, jnp.float32
+    half = width // 2
+    vmem = pl.BlockSpec(memory_space=pltpu.VMEM)
+    return pl.pallas_call(
+        scatter_kernel,
+        out_shape=(
+            jax.ShapeDtypeStruct((rows, width), f32),
+            jax.ShapeDtypeStruct(small.shape, f32),
+        ),
+        in_specs=[vmem, vmem],
+        out_specs=(vmem, vmem),
+        scratch_shapes=[
+            pltpu.VMEM((2, 2, 2, 2, rows, width), bf16),
+            pltpu.VMEM((2, 2, 2, 2, rows, half), bf16),
+            pltpu.VMEM((2, 2, rows, width), bf16),
+            pltpu.VMEM((2, rows, width), bf16),
+            pltpu.VMEM((2, 2, 2, 2, rows, width), bf16),
+            pltpu.VMEM((2, 2, 2, rows, half), bf16),
+            pltpu.VMEM((2, 2, 2, rows, half), bf16),
+            pltpu.VMEM((2, 2, rows, half), bf16),
+            pltpu.VMEM((2, 2, rows, half), bf16),
+            pltpu.VMEM((2, rows, width), bf16),
+            pltpu.VMEM((rows, width), bf16),
+            pltpu.VMEM((5,) + small.shape, f32),
+            pltpu.VMEM((5,) + small.shape, f32),
+            pltpu.SemaphoreType.DMA((12,)),
+            pltpu.SemaphoreType.DMA((12,)),
+        ],
+        compiler_params=pltpu.CompilerParams(
+            collective_id=1, has_side_effects=True, vmem_limit_bytes=40 * 2**20
+        ),
+        cost_estimate=pl.CostEstimate(
+            flops=0, bytes_accessed=120 * 2**20, transcendentals=0
+        ),
+    )(grad.reshape(2, 2, 2, 2, 2, rows, width), small)
 
 
 def shards(
@@ -82,7 +314,16 @@
     capacity = 2 * max(1, count // experts)
     reach = (bucket_table.shape[0] - 1) // 2
     scale = head_dim ** (-0.5)
-    mixer = lax.all_gather(mixer_weight, ("dp", "expert"), axis=0, tiled=True)
+    cube = (
+        lax.axis_size("dp") == 2
+        and lax.axis_size("expert") == 16
+        and mixer_weight.shape[0] % 16 == 0
+        and width % 256 == 0
+    )
+    if cube:
+        mixer = gather_mixer(mixer_weight)
+    else:
+        mixer = lax.all_gather(mixer_weight, ("dp", "expert"), axis=0, tiled=True)
     inner_all, outer_all = (
         lax.all_gather(expert_in, "dp", axis=1, tiled=True),
         lax.all_gather(expert_out, "dp", axis=1, tiled=True),
@@ -140,12 +381,15 @@
     input_part = contract_last(hidden_grad, w_inner).astype(bf16)
     outer_grad = contract_first(grad_arrived, active_low)
     inner_grad = contract_first(arrived, hidden_grad)
+    results = collect(
+        jnp.concatenate([partial_rows, input_part], axis=1), experts, capacity, 2 * width
+    )
+    results, inner_grad, outer_grad = lax.optimization_barrier(
+        (results, inner_grad, outer_grad)
+    )
     inner_share, outer_share = (
         lax.psum_scatter(inner_grad[None], "dp", scatter_dimension=1, tiled=True),
         lax.psum_scatter(outer_grad[None], "dp", scatter_dimension=1, tiled=True),
-    )
-    results = collect(
-        jnp.concatenate([partial_rows, input_part], axis=1), experts, capacity, 2 * width
     )
     tok_both = jnp.dot(place, results[0], preferred_element_type=f32) + jnp.dot(
         place, results[1], preferred_element_type=f32
@@ -190,15 +434,18 @@
     norm_one_grad = jnp.dot(qkv_grad, mixer[: 3 * width], preferred_element_type=f32)
     input_part_one, gain_attn_local = norm_one_back(norm_one_grad)
     tokens_grad = mid_grad + input_part_one
-    mixer_grad = lax.psum_scatter(
-        jnp.concatenate([in_block_grad, out_block_grad], axis=0).astype(bf16),
-        ("dp", "expert"),
-        scatter_dimension=0,
-        tiled=True,
-    ).astype(f32)
+    stacked = jnp.concatenate([in_block_grad.astype(bf16), out_block_grad.astype(bf16)], axis=0)
     pieces = (bias_local, gain_attn_local, gain_ffn_local, router_local)
     flat = jnp.concatenate([piece.reshape(-1) for piece in pieces])
-    total = lax.psum(flat.reshape(-1, 128), ("dp", "expert")).reshape(-1)
+    flat = jnp.pad(flat, (0, -flat.shape[0] % 1024)).reshape(-1, 128)
+    if cube:
+        mixer_grad, total = scatter_mixer(stacked, flat)
+    else:
+        mixer_grad = lax.psum_scatter(
+            stacked, ("dp", "expert"), scatter_dimension=0, tiled=True
+        ).astype(f32)
+        total = lax.psum(flat, ("dp", "expert"))
+    total = total.reshape(-1)
     sums, start = [], 0
     for piece in pieces:
         sums.append(total[start : start + piece.size].reshape(piece.shape))

time: 348 us -> 246 us (0.71)
  waiting for transfers between devices: 207 us -> 60 us
  Pallas kernels: 0 us -> 99.3 us
  blocking collectives: 43.1 us -> 0 us
  other arithmetic: 12.7 us -> 7.68 us
  matrix products: 47 us -> 42.9 us
    pallas_call x0 -> x2, Pallas kernels: none -> 99.3 us  [the longest x1 49.9 us: scatter_mixer(): pl.pallas_call(scatter_kernel, out_shape=(jax.ShapeDtypeStruct((rows, wid...]
    all_gather x1 -> x0, waiting for transfers between devices: 63 us -> none  [shards(): mixer = lax.all_gather(mixer_weight, ('dp', 'expert'), axis=0, tiled=True)]
    reduce_scatter x1 -> x0, waiting for transfers between devices: 46.4 us -> none  [shards(): lax.psum_scatter(jnp.concatenate([in_block_grad, out_block_grad], axis=0)...]
    psum x1 -> x0, blocking collectives: 43.1 us -> none  [shards(): total = lax.psum(flat.reshape(-1, 128), ('dp', 'expert')).reshape(-1)]
    reduce_scatter x1, waiting for transfers between devices: 16.5 us -> 0.01 us  [shards(): lax.psum_scatter(outer_grad[None], 'dp', scatter_dimension=1, tiled=True)]
    reduce_scatter x1, waiting for transfers between devices: 13 us -> 0.01 us  [shards(): lax.psum_scatter(inner_grad[None], 'dp', scatter_dimension=1, tiled=True)]
    all_to_all x1, waiting for transfers between devices: 32.3 us -> 24.6 us  [collect(): lax.all_to_all(results, 'expert', split_axis=0, concat_axis=0, tiled=True)]
  transfers between devices with their start and end apart: 8 -> 6, of which waited for: 6 -> 2; matrix products, arithmetic and copies ran while one was open for 12% -> 19% of each run, Pallas kernels for 0% -> 40%
where the time goes in v2:
time: 246 us
  Pallas kernels  99.3 us (40%)
  waiting for transfers between devices  60 us (24%)
  matrix products  42.9 us (17%)
  between operations  14.7 us (6%)
  starting transfers between devices  12.6 us (5%)
  local copies, waits for them, and re-layouts  8.43 us (3%)
  other arithmetic  7.68 us (3%)
    pallas_call x1, Pallas kernels, scatter_mixer(): pl.pallas_call(scatter_kernel, out_shape=(jax.ShapeDtypeStruct((rows, wid...  49.9 us
    pallas_call x1, Pallas kernels, gather_mixer(): pl.pallas_call(gather_kernel, out_shape=jax.ShapeDtypeStruct((2, 2, 2, 2,...  49.4 us
    all_to_all x1, waiting for transfers between devices, deliver(): lax.all_to_all(doubled.reshape(2 * experts * capacity, width), 'expert',...  33.4 us
    all_to_all x1, waiting for transfers between devices, collect(): lax.all_to_all(results, 'expert', split_axis=0, concat_axis=0, tiled=True)  24.6 us
    dot_general x5, matrix products, contract_last(): lax.dot_general(left, right, (((1,), (1,)), ((), ())), preferred_element_...  11.8 us
    dot_general x6, matrix products, contract_first(): lax.dot_general(left, right, (((0,), (0,)), ((), ())), preferred_element_...  11.3 us
    all_to_all x1, starting transfers between devices, collect(): lax.all_to_all(results, 'expert', split_axis=0, concat_axis=0, tiled=True)  8.28 us
  transfers between devices with their start and end apart: 6, of which 2 were waited for; matrix products, arithmetic and copies ran while one was open for 19% of the time, Pallas kernels for 40%

profile of v2, /device:TPU:0, one launch (start us, length us, event | category | flops | bytes accessed | tf_op | source)
XLA Modules:
  0.0 245.6 jit_solution(10785649179007397733)
XLA Ops:
  7.2 0.7 all-gather.3.cloned.1.call-update
  7.9 1.0 fusion.52
  9.0 0.8 broadcast_compare_fusion
  9.8 0.8 select_reduce_fusion
  10.7 0.3 reshape.200
  11.1 0.6 copy-done.15
  11.7 1.4 fusion.22
  13.2 0.4 copy.54
  13.6 49.4 %shard_map.187 = bf16[2,2,2,2,2,96,768]{6,5,4,3,2,1,0:T(8,128)(2,1)} custom-call(bf16[96,768]{1,0:T(8,128)(2,1)} %own_ref.1), custom_call_target="tpu_custom_call" | custom-call | tf_op jit(solution)/shard_map/pallas_call | solution.py:127
  63.0 3.3 %convolution_convert_fusion.1 = bf16[128,2304]{1,0:T(8,128)(2,1)S(1)} fusion(bf16[3072,768]{1,0:T(8,128)(2,1)} %bitcast.92, bf16[128,768]{1,0:T(8,128)(2,1)S(1)} %copy-done.8, f32[768]{0:T(1024)S(1)} %copy-done.27, f32[128]{0:T(128)S(1)} %fusion.79), kind=kOutput, calls=%fused_computation.5 | convolution fusion | flops 453672960 | bytes 4328960 | tf_op jit(solution)/shard_map/dot_general | solution.py:29
  66.9 0.3 fusion.32
  67.2 1.2 fusion.88
  68.4 0.3 convolution_convert_fusion.8
  68.8 2.0 multiply_reduce_fusion.3
  71.4 0.5 copy-done.37
  72.0 0.5 convolution_convert_fusion.2
  72.5 1.3 broadcast_in_dim.50
  73.8 4.0 %all-to-all-start = ((bf16[16,32,1536]{2,1,0:T(8,128)(2,1)}), bf16[16,32,1536]{2,1,0:T(8,128)(2,1)S(1)}, u32[]{:S(2)}, u32[]{:S(2)}) async-start(bf16[16,32,1536]{2,1,0:T(8,128)(2,1)} %bitcast.13), calls=%async_computation | async-start | bytes 3145728 | tf_op jit(solution)/shard_map/all_to_all | solution.py:48
  77.9 0.7 all-gather.5.cloned.1.call-update
  78.6 33.4 %all-to-all-done = bf16[16,32,1536]{2,1,0:T(8,128)(2,1)S(1)} async-done(((bf16[16,32,1536]{2,1,0:T(8,128)(2,1)}), bf16[16,32,1536]{2,1,0:T(8,128)(2,1)S(1)}, u32[]{:S(2)}, u32[]{:S(2)}) %all-to-all-start) | async-done | bytes 1572896 | tf_op jit(solution)/shard_map/all_to_all | solution.py:48
  112.0 4.7 %fusion.19 = f32[512,1536]{1,0:T(8,128)} fusion(bf16[1,768,1536]{2,1,0:T(8,128)(2,1)} %all-gather.3.cloned.1.call-done, bf16[512,1536]{1,0:T(8,128)(2,1)S(1)} %bitcast.98), kind=kOutput, calls=%fused_computation.25 | convolution fusion | flops 1207959552 | bytes 6291456 | tf_op jit(solution)/shard_map/dot_general | solution.py:375
  116.8 4.7 %fusion.27 = bf16[512,768]{1,0:T(8,128)(2,1)S(1)} fusion(bf16[1,768,1536]{2,1,0:T(8,128)(2,1)} %all-gather.5.cloned.1.call-done, f32[512,1536]{1,0:T(8,128)} %fusion.19), kind=kOutput, calls=%fused_computation.34 | convolution fusion | flops 1215430656 | bytes 6291456 | tf_op jit(solution)/shard_map/dot_general | solution.py:29
  121.5 2.8 %fusion.7 = bf16[512,1536]{1,0:T(8,128)(2,1)S(1)} fusion(f32[512,1536]{1,0:T(8,128)S(1)} %copy-done.47, bf16[1,768,1536]{2,1,0:T(8,128)(2,1)S(1)} %copy-done.44, bf16[512,1536]{1,0:T(8,128)(2,1)S(1)} %bitcast.99), kind=kOutput, calls=%fused_computation.12 | convolution fusion | flops 1223688192 | bytes 7864320 | tf_op jit(solution)/shard_map/dot_general | solution.py:379
  124.3 1.4 fusion.24
  125.8 1.3 pad_maximum_fusion.1
  127.0 8.3 %all-to-all-start.1 = ((bf16[16,32,1536]{2,1,0:T(8,128)(2,1)}), bf16[16,32,1536]{2,1,0:T(8,128)(2,1)S(1)}, u32[]{:S(2)}, u32[]{:S(2)}) async-start(bf16[16,32,1536]{2,1,0:T(8,128)(2,1)} %bitcast.17), calls=%async_computation.1 | async-start | bytes 3145728 | tf_op jit(solution)/shard_map/all_to_all | solution.py:58
  135.6 5.2 %fusion.42 = f32[768,1536]{1,0:T(8,128)} fusion(bf16[512,1536]{1,0:T(8,128)(2,1)} %copy-done.14, bf16[512,1536]{1,0:T(8,128)(2,1)S(1)} %bitcast.100), kind=kOutput, calls=%fused_computation.63 | convolution fusion | flops 1207959552 | bytes 7077888 | tf_op jit(solution)/shard_map/dot_general | solution.py:23
  140.7 3.8 %fusion.39 = f32[768,1536]{1,0:T(8,128)} fusion(bf16[512,1536]{1,0:T(8,128)(2,1)S(1)} %bitcast.101, f32[512,1536]{1,0:T(8,128)S(1)} %copy-done.48), kind=kOutput, calls=%fused_computation.60 | convolution fusion | flops 1215037440 | bytes 8650752 | tf_op jit(solution)/shard_map/dot_general | solution.py:23
  144.5 24.6 %all-to-all-done.1 = bf16[16,32,1536]{2,1,0:T(8,128)(2,1)S(1)} async-done(((bf16[16,32,1536]{2,1,0:T(8,128)(2,1)}), bf16[16,32,1536]{2,1,0:T(8,128)(2,1)S(1)}, u32[]{:S(2)}, u32[]{:S(2)}) %all-to-all-start.1) | async-done | bytes 1572896 | tf_op jit(solution)/shard_map/all_to_all | solution.py:58
  169.4 0.5 reduce-scatter.5.cloned.1.call-update
  170.0 0.3 fusion.59
  170.9 0.8 fusion.50
  172.2 0.4 multiply_reduce_fusion.1
  172.8 1.6 convolution_convert_fusion.7
  174.6 0.3 multiply_reduce_fusion
  175.1 0.5 copy.60
  175.6 1.2 fusion.33
  176.9 1.9 convolution_convert_fusion.4
  178.8 0.4 convolution_convert_fusion.5
  179.5 3.7 %fusion.48 = (f32[768]{0:T(1024)S(1)}, f32[128]{0:T(128)S(1)}, f32[128,768]{1,0:T(8,128)S(1)}) fusion(bf16[128,768]{1,0:T(8,128)(2,1)S(1)} %copy-done.9, f32[128]{0:T(128)S(1)} %copy-done.40, f32[768]{0:T(1024)S(1)} %copy-done.28, bf16[3072,768]{1,0:T(8,128)(2,1)} %bitcast.95, bf16[128,768]{0,1:T(8,128)(2,1)S(1)} %bitcast.120, ...), kind=kOutput, calls=%fused_computation.75 | convolution fusion | flops 455441536 | bytes 4725760 | tf_op jit(solution)/shard_map/dot_general | solution.py:434
  183.2 0.5 convolution_convert_fusion.3
  183.7 1.1 convolution_convert_fusion
  185.2 49.9 %shard_map.188 = (f32[96,768]{1,0:T(8,128)S(1)}, f32[64,128]{1,0:T(8,128)S(1)}) custom-call(bf16[2,2,2,2,2,96,768]{6,5,4,3,2,1,0:T(8,128)(2,1)S(1)} %bitcast.90, f32[64,128]{1,0:T(8,128)S(1)} %fusion.67.small_ref), custom_call_target="tpu_custom_call" | custom-call | bytes 125829120 | tf_op jit(solution)/shard_map/pallas_call | solution.py:259
  235.2 0.7 copy.63
  236.1 0.7 copy.64
  236.9 0.6 slice_bitcast_fusion
  237.5 0.9 fusion.51
  238.4 0.7 copy.74
  (142 shorter events, 4.4 us)
Async XLA Ops:
  7.2 63.7 %copy-start = (bf16[768,8]{0,1:T(8,128)(2,1)S(1)}, bf16[768,8]{0,1:T(8,128)(2,1)}, u32[]{:S(2)}) copy-start(bf16[768,8]{0,1:T(8,128)(2,1)} %param.21) | copy-start | bytes 36868
  7.2 71.4 %all-gather.3.cloned.1.call-start = ((), (), s32[]{:S(2)}) async-start(), calls=%async_computation.4 | async-start | bytes 3538944 | tf_op jit(solution)/shard_map/all_gather | solution.py:328
  9.0 54.0 %copy-start.39 = (f32[128]{0:T(128)}, f32[128]{0:T(128)S(1)}, u32[]{:S(2)}) copy-start(f32[128]{0:T(128)S(1)} %fusion.79) | copy-start | bytes 1540
  13.2 49.8 %copy-start.8 = (bf16[128,768]{1,0:T(8,128)(2,1)S(1)}, bf16[128,768]{1,0:T(8,128)(2,1)}, u32[]{:S(2)}) copy-start(bf16[128,768]{1,0:T(8,128)(2,1)} %param.12) | copy-start | bytes 589828
  13.2 49.8 %copy-start.27 = (f32[768]{0:T(1024)S(1)}, f32[768]{0:T(1024)}, u32[]{:S(2)}) copy-start(f32[768]{0:T(1024)} %param.19) | copy-start | bytes 9220
  66.5 1.9 copy-start.10
  66.7 2.0 copy-start.12
  66.9 1.9 copy-start.19
  67.2 3.5 %copy-start.1 = (f32[12,128,128]{1,2,0:T(8,128)}, f32[12,128,128]{1,2,0:T(8,128)S(1)}, u32[]{:S(2)}) copy-start(f32[12,128,128]{1,2,0:T(8,128)S(1)} %fusion.32) | copy-start | bytes 2359300
  68.4 2.7 %copy-start.23 = (f32[12,128]{1,0:T(8,128)}, f32[12,128]{1,0:T(8,128)S(1)}, u32[]{:S(2)}) copy-start(f32[12,128]{1,0:T(8,128)S(1)} %get-tuple-element.61) | copy-start | bytes 18436
  68.4 2.4 copy-start.21
  68.4 2.8 %copy-start.31 = (s32[128,1]{0,1:T(1,128)S(1)}, s32[128,1]{0,1:T(1,128)}, u32[]{:S(2)}) copy-start(s32[128,1]{0,1:T(1,128)} %param.15) | copy-start | bytes 1540
  68.4 3.5 %copy-start.5 = (bf16[128,768]{1,0:T(8,128)(2,1)S(1)}, bf16[128,768]{1,0:T(8,128)(2,1)}, u32[]{:S(2)}) copy-start(bf16[128,768]{1,0:T(8,128)(2,1)} %param.13) | copy-start | bytes 589828
  68.8 5.0 %copy-start.17 = (bf16[12,64,128]{2,1,0:T(8,128)(2,1)}, bf16[12,64,128]{2,1,0:T(8,128)(2,1)S(1)}, u32[]{:S(2)}) copy-start(bf16[12,64,128]{2,1,0:T(8,128)(2,1)S(1)} %convolution_convert_fusion.8) | copy-start | bytes 589828
  70.8 3.0 %copy-start.45 = (f32[128]{0:T(128)}, f32[128]{0:T(128)S(1)}, u32[]{:S(2)}) copy-start(f32[128]{0:T(128)S(1)} %get-tuple-element.63) | copy-start | bytes 1540
  70.9 1.1 copy-start.3
  71.1 2.7 %copy-start.25 = (f32[128]{0:T(128)}, f32[128]{0:T(128)S(1)}, u32[]{:S(2)}) copy-start(f32[128]{0:T(128)S(1)} %get-tuple-element.65) | copy-start | bytes 1540
  71.2 2.6 %copy-start.29 = (f32[128]{0:T(128)}, f32[128]{0:T(128)S(1)}, u32[]{:S(2)}) copy-start(f32[128]{0:T(128)S(1)} %fusion.74) | copy-start | bytes 1540
  71.9 1.9 copy-start.35
  73.8 38.2 %all-to-all-start = ((bf16[16,32,1536]{2,1,0:T(8,128)(2,1)}), bf16[16,32,1536]{2,1,0:T(8,128)(2,1)S(1)}, u32[]{:S(2)}, u32[]{:S(2)}) async-start(bf16[16,32,1536]{2,1,0:T(8,128)(2,1)} %bitcast.13), calls=%async_computation | async-start | bytes 3145728 | tf_op jit(solution)/shard_map/all_to_all | solution.py:48
  77.8 39.0 %all-gather.5.cloned.1.call-start = ((), (), s32[]{:S(2)}) async-start(), calls=%async_computation.5 | async-start | bytes 3538944 | tf_op jit(solution)/shard_map/all_gather | solution.py:329
  116.8 4.7 %copy-start.44 = (bf16[1,768,1536]{2,1,0:T(8,128)(2,1)S(1)}, bf16[1,768,1536]{2,1,0:T(8,128)(2,1)}, u32[]{:S(2)}) copy-start(bf16[1,768,1536]{2,1,0:T(8,128)(2,1)} %all-gather.5.cloned.1.call-done) | copy-start | bytes 7077892
  116.8 4.7 %copy-start.47 = (f32[512,1536]{1,0:T(8,128)S(1)}, f32[512,1536]{1,0:T(8,128)}, u32[]{:S(2)}) copy-start(f32[512,1536]{1,0:T(8,128)} %fusion.19) | copy-start | bytes 9437188
  121.5 2.8 %copy-start.43 = (bf16[1,768,1536]{2,1,0:T(8,128)(2,1)S(1)}, bf16[1,768,1536]{2,1,0:T(8,128)(2,1)}, u32[]{:S(2)}) copy-start(bf16[1,768,1536]{2,1,0:T(8,128)(2,1)} %all-gather.3.cloned.1.call-done) | copy-start | bytes 7077892
  124.3 1.4 copy-start.14
  127.0 42.1 %all-to-all-start.1 = ((bf16[16,32,1536]{2,1,0:T(8,128)(2,1)}), bf16[16,32,1536]{2,1,0:T(8,128)(2,1)S(1)}, u32[]{:S(2)}, u32[]{:S(2)}) async-start(bf16[16,32,1536]{2,1,0:T(8,128)(2,1)} %bitcast.17), calls=%async_computation.1 | async-start | bytes 3145728 | tf_op jit(solution)/shard_map/all_to_all | solution.py:58
  135.3 103.0 %reduce-scatter.3.cloned.1.call-start = ((), (), s32[]{:S(2)}) async-start(), calls=%async_computation.6 | async-start | bytes 7077888 | tf_op jit(solution)/shard_map/reduce_scatter | solution.py:391
  135.5 5.2 %copy-start.48 = (f32[512,1536]{1,0:T(8,128)S(1)}, f32[512,1536]{1,0:T(8,128)}, u32[]{:S(2)}) copy-start(f32[512,1536]{1,0:T(8,128)} %fusion.19) | copy-start | bytes 9437188
  169.3 69.1 %reduce-scatter.5.cloned.1.call-start = ((), (), s32[]{:S(2)}) async-start(), calls=%async_computation.7 | async-start | bytes 7077888 | tf_op jit(solution)/shard_map/reduce_scatter | solution.py:392
  169.9 0.9 copy-start.38
  169.9 1.7 copy-start.26
  169.9 1.7 copy-start.32
  170.0 1.8 copy-start.4
  170.0 2.2 copy-start.22
  170.0 2.2 copy-start.34
  170.3 2.3 copy-start.46
  170.3 2.3 copy-start.7
  171.7 2.9 %copy-start.2 = (f32[12,128,128]{1,2,0:T(8,128)S(1)}, f32[12,128,128]{1,2,0:T(8,128)}, u32[]{:S(2)}) copy-start(f32[12,128,128]{1,2,0:T(8,128)} %get-tuple-element.62) | copy-start | bytes 2359300
  171.7 2.9 %copy-start.20 = (bf16[128,768]{0,1:T(8,128)(2,1)S(1)}, bf16[128,768]{0,1:T(8,128)(2,1)}, u32[]{:S(2)}) copy-start(bf16[128,768]{0,1:T(8,128)(2,1)} %copy-done.19) | copy-start | bytes 589828
  171.7 2.9 %copy-start.24 = (f32[12,128]{1,0:T(8,128)S(1)}, f32[12,128]{1,0:T(8,128)}, u32[]{:S(2)}) copy-start(f32[12,128]{1,0:T(8,128)} %copy-done.23) | copy-start | bytes 18436
  174.6 1.0 copy-start.16
  175.1 3.8 %copy-start.13 = (bf16[128,768]{0,1:T(8,128)(2,1)S(1)}, bf16[128,768]{0,1:T(8,128)(2,1)}, u32[]{:S(2)}) copy-start(bf16[128,768]{0,1:T(8,128)(2,1)} %copy-done.12) | copy-start | bytes 589828
  175.6 3.6 %copy-start.11 = (bf16[128,768]{0,1:T(8,128)(2,1)S(1)}, bf16[128,768]{0,1:T(8,128)(2,1)}, u32[]{:S(2)}) copy-start(bf16[128,768]{0,1:T(8,128)(2,1)} %copy-done.10) | copy-start | bytes 589828
  176.8 2.7 %copy-start.9 = (bf16[128,768]{1,0:T(8,128)(2,1)S(1)}, bf16[128,768]{1,0:T(8,128)(2,1)}, u32[]{:S(2)}) copy-start(bf16[128,768]{1,0:T(8,128)(2,1)} %param.12) | copy-start | bytes 589828
  176.8 2.7 %copy-start.28 = (f32[768]{0:T(1024)S(1)}, f32[768]{0:T(1024)}, u32[]{:S(2)}) copy-start(f32[768]{0:T(1024)} %param.19) | copy-start | bytes 9220
  176.8 2.7 %copy-start.40 = (f32[128]{0:T(128)S(1)}, f32[128]{0:T(128)}, u32[]{:S(2)}) copy-start(f32[128]{0:T(128)} %copy-done.39) | copy-start | bytes 1540
  179.5 3.7 %copy-start.18 = (bf16[12,64,128]{2,1,0:T(8,128)(2,1)S(1)}, bf16[12,64,128]{2,1,0:T(8,128)(2,1)}, u32[]{:S(2)}) copy-start(bf16[12,64,128]{2,1,0:T(8,128)(2,1)} %copy-done.17) | copy-start | bytes 589828
  185.2 51.7 %copy-start.42 = (f32[128]{0:T(128)S(1)}, f32[128]{0:T(128)}, u32[]{:S(2)}) copy-start(f32[128]{0:T(128)} %copy-done.41) | copy-start | bytes 1540
  (7 other events, 4.9 us)
Sparse Core Ops, SparseCore 0:
  9.6 13.6 all-gather.2
  80.2 12.2 all-gather.4
  169.4 14.2 reduce-scatter.2
  186.6 13.8 reduce-scatter.4

commit v3 on v2

--- a/solution.py
+++ b/solution.py
@@ -290,6 +290,97 @@
     )(grad.reshape(2, 2, 2, 2, 2, rows, width), small)
 
 
+AWAY = (4, 3, 5, 2, 6, 1, 7)
+
+
+def planes():
+    core, chip = lax.axis_index("dp"), lax.axis_index("expert")
+    expert, side = chip // 2, chip % 2
+    peers = {step: (core, ((expert + step) % 8) * 2 + side) for step in AWAY}
+    return expert, side, (core, chip + 1 - 2 * side), peers
+
+
+def remote(source, target_ref, sems, number, target):
+    copy = pltpu.make_async_remote_copy(
+        src_ref=source,
+        dst_ref=target_ref,
+        send_sem=sems[0].at[number],
+        recv_sem=sems[1].at[number],
+        device_id=target,
+        device_id_type=MESH,
+    )
+    copy.start()
+    return copy
+
+
+def dispatch_kernel(rows_ref, out_ref, local_sem, *sems):
+    expert, side, twin, peers = planes()
+    local = pltpu.make_async_copy(rows_ref.at[expert], out_ref.at[side, expert], local_sem)
+    local.start()
+    meet([twin] + [peers[step] for step in AWAY])
+    out = {
+        step: remote(
+            rows_ref.at[(expert + step) % 8], out_ref.at[side, expert], sems, step, peers[step]
+        )
+        for step in AWAY
+    }
+    local.wait()
+    across = [remote(out_ref.at[side, expert], out_ref.at[side, expert], sems, 8, twin)]
+    for step in AWAY:
+        out[step].wait_recv()
+        origin = (expert + 8 - step) % 8
+        block = out_ref.at[side, origin]
+        across.append(remote(block, block, sems, 8 + step, twin))
+    for copy in across:
+        copy.wait_recv()
+    for copy in list(out.values()) + across:
+        copy.wait_send()
+
+
+def collect_kernel(part_ref, out_ref, arrived, summed, *sems):
+    expert, side, twin, peers = planes()
+    meet([twin] + [peers[step] for step in AWAY])
+    order = AWAY + (0,)
+    across = {}
+    for step in order:
+        goal = (expert + step) % 8
+        across[step] = remote(part_ref.at[1 - side, goal], arrived.at[goal], sems, step, twin)
+    out = []
+    for step in order:
+        goal = (expert + step) % 8
+        across[step].wait_recv()
+        total = part_ref[side, goal].astype(jnp.float32) + arrived[goal].astype(jnp.float32)
+        total = total.astype(out_ref.dtype)
+        if step == 0:
+            out_ref[goal] = total
+        else:
+            summed[goal] = total
+            out.append(
+                remote(summed.at[goal], out_ref.at[expert], sems, 8 + step, peers[step])
+            )
+    for copy in out:
+        copy.wait_recv()
+    for copy in out + list(across.values()):
+        copy.wait_send()
+
+
+def exchange(kernel, number, value, result, scratch, local):
+    vmem = pl.BlockSpec(memory_space=pltpu.VMEM)
+    return pl.pallas_call(
+        kernel,
+        out_shape=jax.ShapeDtypeStruct(result, value.dtype),
+        in_specs=[vmem],
+        out_specs=vmem,
+        scratch_shapes=[pltpu.VMEM(result, value.dtype)] * scratch
+        + [pltpu.SemaphoreType.DMA] * local
+        + [pltpu.SemaphoreType.DMA((16,))] * 2,
+        compiler_params=pltpu.CompilerParams(
+            collective_id=number, has_side_effects=True, vmem_limit_bytes=24 * 2**20
+        ),
+        cost_estimate=pl.CostEstimate(flops=0, bytes_accessed=60 * 2**20, transcendentals=0),
+    )(value)
+
+
 def shards(
     tokens,
     cotangent,
@@ -370,7 +461,18 @@
     expert_grad_tok = (gate[:, None] * upstream).astype(bf16)
     both = jnp.concatenate([normed_two, expert_grad_tok], axis=1)
     buffer = contract_first(place, both).astype(bf16)
-    arrived_both = deliver(buffer, experts, capacity, 2 * width)
+    direct = cube and experts == 8 and capacity % 16 == 0
+    if direct:
+        arrived_both = exchange(
+            dispatch_kernel,
+            2,
+            buffer.reshape(8, capacity, 2 * width),
+            (2, 8, capacity, 2 * width),
+            0,
+            1,
+        ).reshape(16 * capacity, 2 * width)
+    else:
+        arrived_both = deliver(buffer, experts, capacity, 2 * width)
     arrived, grad_arrived = arrived_both[:, :width], arrived_both[:, width:]
     hidden = jnp.dot(arrived, w_inner, preferred_element_type=f32)
     active, active_back = jax.vjp(tanh_gelu, hidden)
@@ -381,9 +483,20 @@
     input_part = contract_last(hidden_grad, w_inner).astype(bf16)
     outer_grad = contract_first(grad_arrived, active_low)
     inner_grad = contract_first(arrived, hidden_grad)
-    results = collect(
-        jnp.concatenate([partial_rows, input_part], axis=1), experts, capacity, 2 * width
-    )
+    part = jnp.concatenate([partial_rows, input_part], axis=1)
+    if direct:
+        results = [
+            exchange(
+                collect_kernel,
+                3,
+                part.reshape(2, 8, capacity, 2 * width),
+                (8, capacity, 2 * width),
+                2,
+                0,
+            ).reshape(8 * capacity, 2 * width)
+        ]
+    else:
+        results = collect(part, experts, capacity, 2 * width)
     results, inner_grad, outer_grad = lax.optimization_barrier(
         (results, inner_grad, outer_grad)
     )
@@ -391,9 +504,7 @@
         lax.psum_scatter(inner_grad[None], "dp", scatter_dimension=1, tiled=True),
         lax.psum_scatter(outer_grad[None], "dp", scatter_dimension=1, tiled=True),
     )
-    tok_both = jnp.dot(place, results[0], preferred_element_type=f32) + jnp.dot(
-        place, results[1], preferred_element_type=f32
-    )
+    tok_both = sum(jnp.dot(place, rows, preferred_element_type=f32) for rows in results)
     expert_tok, input_tok = tok_both[:, :width], tok_both[:, width:]
     mixed = (x_mid + gate[:, None] * expert_tok).astype(bf16)
     gate_grad = jnp.sum(upstream * expert_tok, axis=1)

time: 246 us -> 224 us (0.911)
  waiting for transfers between devices: 60 us -> 1.72 us
  Pallas kernels: 99.3 us -> 152 us
  starting transfers between devices: 12.6 us -> 0.38 us
    all_to_all x2 -> x0, waiting for transfers between devices: 58 us -> none  [the longest x1 33.4 us: deliver(): lax.all_to_all(doubled.reshape(2 * experts * capacity, width), 'expert',...]
    pallas_call x0 -> x2, Pallas kernels: none -> 55.2 us  [exchange(): pl.pallas_call(kernel, out_shape=jax.ShapeDtypeStruct(result, value.dtype...]
    all_to_all x2 -> x0, starting transfers between devices: 12.3 us -> none  [the longest x1 8.28 us: collect(): lax.all_to_all(results, 'expert', split_axis=0, concat_axis=0, tiled=True)]
    dot_general x5, matrix products: 11.8 us -> 9.06 us  [contract_last(): lax.dot_general(left, right, (((1,), (1,)), ((), ())), preferred_element_...]
  transfers between devices with their start and end apart: 6 -> 4, of which waited for: 2 -> 0; matrix products, arithmetic and copies ran while one was open for 19% -> 18% of each run, Pallas kernels for 40% -> 58%
where the time goes in v3:
time: 224 us
  Pallas kernels  152 us (68%)
  matrix products  40.5 us (18%)
  between operations  14.4 us (6%)
  local copies, waits for them, and re-layouts  8.23 us (4%)
  other arithmetic  6.5 us (3%)
    pallas_call x2, Pallas kernels, exchange(): pl.pallas_call(kernel, out_shape=jax.ShapeDtypeStruct(result, value.dtype...  55.2 us
    pallas_call x1, Pallas kernels, gather_mixer(): pl.pallas_call(gather_kernel, out_shape=jax.ShapeDtypeStruct((2, 2, 2, 2,...  49.4 us
    pallas_call x1, Pallas kernels, scatter_mixer(): pl.pallas_call(scatter_kernel, out_shape=(jax.ShapeDtypeStruct((rows, wid...  47.7 us
    dot_general x6, matrix products, contract_first(): lax.dot_general(left, right, (((0,), (0,)), ((), ())), preferred_element_...  10.5 us
    dot_general x5, matrix products, contract_last(): lax.dot_general(left, right, (((1,), (1,)), ((), ())), preferred_element_...  9.06 us
    dot_general x1, matrix products, shards(): active_grad = jnp.dot(grad_arrived, w_outer, preferred_element_type=f32)  4.93 us
  transfers between devices with their start and end apart: 4, of which 0 were waited for; matrix products, arithmetic and copies ran while one was open for 18% of the time, Pallas kernels for 58%

profile of v3, /device:TPU:0, one launch (start us, length us, event | category | flops | bytes accessed | tf_op | source)
XLA Modules:
  0.0 224.0 jit_solution(15249800924804892301)
XLA Ops:
  7.2 0.7 all-gather.3.cloned.1.call-update
  8.0 0.7 all-gather.5.cloned.1.call-update
  8.7 1.0 fusion.52
  9.8 0.8 broadcast_compare_fusion
  10.6 0.8 select_reduce_fusion
  11.5 0.3 reshape.200
  11.9 0.8 fusion.22
  12.7 0.4 copy.54
  13.0 49.4 %shard_map.187 = bf16[2,2,2,2,2,96,768]{6,5,4,3,2,1,0:T(8,128)(2,1)} custom-call(bf16[96,768]{1,0:T(8,128)(2,1)} %own_ref.1), custom_call_target="tpu_custom_call" | custom-call | tf_op jit(solution)/shard_map/pallas_call | solution.py:127
  62.5 3.3 %convolution_convert_fusion.1 = bf16[128,2304]{1,0:T(8,128)(2,1)S(1)} fusion(bf16[3072,768]{1,0:T(8,128)(2,1)} %bitcast.95, bf16[128,768]{1,0:T(8,128)(2,1)S(1)} %copy-done.4, f32[768]{0:T(1024)S(1)} %copy-done.14, f32[128]{0:T(128)S(1)} %fusion.78), kind=kOutput, calls=%fused_computation.5 | convolution fusion | flops 453672960 | bytes 4328960 | tf_op jit(solution)/shard_map/dot_general | solution.py:29
  66.4 0.3 fusion.32
  66.7 1.1 fusion.86
  67.8 0.3 convolution_convert_fusion.8
  68.1 2.0 multiply_reduce_fusion.3
  70.9 0.5 convolution_convert_fusion.2
  71.4 32.3 %shard_map.188 = bf16[2,8,32,1536]{3,2,1,0:T(8,128)(2,1)S(1)} custom-call(bf16[8,32,1536]{2,1,0:T(8,128)(2,1)S(1)} %bitcast.93), custom_call_target="tpu_custom_call" | custom-call | bytes 62914560 | tf_op jit(solution)/shard_map/pallas_call | solution.py:369
  103.7 3.1 %fusion.19 = f32[512,1536]{1,0:T(8,128)S(1)} fusion(bf16[1,768,1536]{2,1,0:T(8,128)(2,1)} %all-gather.3.cloned.1.call-done, bf16[512,1536]{1,0:T(8,128)(2,1)S(1)} %bitcast.88), kind=kOutput, calls=%fused_computation.24 | convolution fusion | flops 1207959552 | bytes 6291456 | tf_op jit(solution)/shard_map/dot_general | solution.py:477
  106.8 1.6 copy-done.23
  108.4 3.7 %fusion.39 = f32[768,1536]{1,0:T(8,128)} fusion(bf16[512,1536]{1,0:T(8,128)(2,1)S(1)} %bitcast.89, f32[512,1536]{1,0:T(8,128)S(1)} %fusion.19), kind=kOutput, calls=%fused_computation.59 | convolution fusion | flops 1215037440 | bytes 8650752 | tf_op jit(solution)/shard_map/dot_general | solution.py:23
  112.2 4.9 %fusion.7 = bf16[512,1536]{1,0:T(8,128)(2,1)S(1)} fusion(f32[512,1536]{1,0:T(8,128)} %copy-done.23, bf16[1,768,1536]{2,1,0:T(8,128)(2,1)} %all-gather.5.cloned.1.call-done, bf16[512,1536]{1,0:T(8,128)(2,1)S(1)} %bitcast.90), kind=kOutput, calls=%fused_computation.12 | convolution fusion | flops 1223688192 | bytes 7864320 | tf_op jit(solution)/shard_map/dot_general | solution.py:481
  117.1 3.7 %fusion.42 = f32[768,1536]{1,0:T(8,128)} fusion(bf16[512,1536]{1,0:T(8,128)(2,1)S(1)} %fusion.7, bf16[512,1536]{1,0:T(8,128)(2,1)S(1)} %bitcast.91), kind=kOutput, calls=%fused_computation.62 | convolution fusion | flops 1207959552 | bytes 7077888 | tf_op jit(solution)/shard_map/dot_general | solution.py:23
  120.8 2.0 fusion.27
  122.8 1.4 fusion.24
  124.3 22.9 %shard_map.189 = bf16[8,32,1536]{2,1,0:T(8,128)(2,1)S(1)} custom-call(bf16[2,8,32,1536]{3,2,1,0:T(8,128)(2,1)S(1)} %bitcast.87), custom_call_target="tpu_custom_call" | custom-call | bytes 62914560 | tf_op jit(solution)/shard_map/pallas_call | solution.py:369
  147.3 0.3 reduce-scatter.5.cloned.1.call-start
  147.5 0.3 reduce-scatter.5.cloned.1.call-update
  147.9 0.3 fusion.59
  148.2 0.8 fusion.50
  149.0 1.0 fusion.88
  150.0 1.2 reshape.212
  151.2 0.4 multiply_reduce_fusion.1
  151.8 1.9 convolution_convert_fusion.7
  153.9 1.4 multiply_reduce_fusion
  155.4 0.5 copy.60
  155.9 1.2 fusion.33
  157.2 2.0 convolution_convert_fusion.4
  159.2 1.3 convolution_convert_fusion.5
  160.5 0.2 convolution_convert_fusion.6
  160.8 3.0 %fusion.48 = (f32[768]{0:T(1024)S(1)}, f32[128]{0:T(128)S(1)}, f32[128,768]{1,0:T(8,128)S(1)}) fusion(bf16[128,768]{1,0:T(8,128)(2,1)S(1)} %copy-done.4, f32[128]{0:T(128)S(1)} %fusion.78, f32[768]{0:T(1024)S(1)} %copy-done.14, bf16[3072,768]{1,0:T(8,128)(2,1)} %bitcast.98, bf16[128,768]{0,1:T(8,128)(2,1)} %bitcast.115, bf16[128,768]{0,1:T(8,128)(2,1)S(1)} %bitcast.104, ...), kind=kOutput, calls=%fused_computation.74 | convolution fusion | flops 455441536 | bytes 4725760 | tf_op jit(solution)/shard_map/dot_general | solution.py:545
  163.8 0.5 convolution_convert_fusion.3
  164.3 1.1 convolution_convert_fusion
  165.4 0.3 pad_maximum_fusion
  165.8 47.7 %shard_map.190 = (f32[96,768]{1,0:T(8,128)S(1)}, f32[64,128]{1,0:T(8,128)S(1)}) custom-call(bf16[2,2,2,2,2,96,768]{6,5,4,3,2,1,0:T(8,128)(2,1)S(1)} %bitcast.86, f32[64,128]{1,0:T(8,128)S(1)} %fusion.66.small_ref), custom_call_target="tpu_custom_call" | custom-call | bytes 125829120 | tf_op jit(solution)/shard_map/pallas_call | solution.py:259
  213.6 0.7 copy.63
  214.5 0.7 copy.64
  215.3 0.6 slice_bitcast_fusion
  215.9 0.9 fusion.51
  216.8 0.7 copy.74
  (89 shorter events, 2.7 us)
Async XLA Ops:
  7.2 63.1 %copy-start = (bf16[768,8]{0,1:T(8,128)(2,1)S(1)}, bf16[768,8]{0,1:T(8,128)(2,1)}, u32[]{:S(2)}) copy-start(bf16[768,8]{0,1:T(8,128)(2,1)} %param.21) | copy-start | bytes 36868
  7.2 4.7 %copy-start.16 = (f32[32,12]{0,1:T(8,128)S(1)}, f32[32,12]{0,1:T(8,128)}, u32[]{:S(2)}) copy-start(f32[32,12]{0,1:T(8,128)} %param.18) | copy-start | bytes 4612
  7.2 96.5 %all-gather.3.cloned.1.call-start = ((), (), s32[]{:S(2)}) async-start(), calls=%async_computation.2 | async-start | bytes 3538944 | tf_op jit(solution)/shard_map/all_gather | solution.py:419
  7.9 104.2 %all-gather.5.cloned.1.call-start = ((), (), s32[]{:S(2)}) async-start(), calls=%async_computation.3 | async-start | bytes 3538944 | tf_op jit(solution)/shard_map/all_gather | solution.py:420
  8.7 208.1 %reduce-scatter.3.cloned.1.call-start = ((), (), s32[]{:S(2)}) async-start(), calls=%async_computation.4 | async-start | bytes 7077888 | tf_op jit(solution)/shard_map/reduce_scatter | solution.py:504
  9.8 52.7 %copy-start.17 = (f32[128]{0:T(128)}, f32[128]{0:T(128)S(1)}, u32[]{:S(2)}) copy-start(f32[128]{0:T(128)S(1)} %fusion.52) | copy-start | bytes 1540
  12.6 49.8 %copy-start.4 = (bf16[128,768]{1,0:T(8,128)(2,1)S(1)}, bf16[128,768]{1,0:T(8,128)(2,1)}, u32[]{:S(2)}) copy-start(bf16[128,768]{1,0:T(8,128)(2,1)} %param.12) | copy-start | bytes 589828
  12.7 49.8 %copy-start.14 = (f32[768]{0:T(1024)S(1)}, f32[768]{0:T(1024)}, u32[]{:S(2)}) copy-start(f32[768]{0:T(1024)} %param.19) | copy-start | bytes 9220
  66.0 1.8 copy-start.5
  66.2 1.9 copy-start.7
  66.4 5.1 %copy-start.10 = (bf16[128,768]{0,1:T(8,128)(2,1)}, bf16[128,768]{0,1:T(8,128)(2,1)S(1)}, u32[]{:S(2)}) copy-start(bf16[128,768]{0,1:T(8,128)(2,1)S(1)} %copy.51) | copy-start | bytes 589828
  67.8 2.4 %copy-start.13 = (f32[768]{0:T(1024)S(1)}, f32[768]{0:T(1024)}, u32[]{:S(2)}) copy-start(f32[768]{0:T(1024)} %param.20) | copy-start | bytes 9220
  67.8 2.9 %copy-start.15 = (s32[128,1]{0,1:T(1,128)S(1)}, s32[128,1]{0,1:T(1,128)}, u32[]{:S(2)}) copy-start(s32[128,1]{0,1:T(1,128)} %param.15) | copy-start | bytes 1540
  67.8 3.1 %copy-start.3 = (bf16[128,768]{1,0:T(8,128)(2,1)S(1)}, bf16[128,768]{1,0:T(8,128)(2,1)}, u32[]{:S(2)}) copy-start(bf16[128,768]{1,0:T(8,128)(2,1)} %param.13) | copy-start | bytes 589828
  68.1 2.0 copy-start.8
  70.1 0.5 copy-start.21
  106.8 1.6 copy-start.23
  117.1 3.7 %copy-start.20 = (bf16[1,768,1536]{2,1,0:T(8,128)(2,1)S(1)}, bf16[1,768,1536]{2,1,0:T(8,128)(2,1)}, u32[]{:S(2)}) copy-start(bf16[1,768,1536]{2,1,0:T(8,128)(2,1)} %all-gather.5.cloned.1.call-done) | copy-start | bytes 7077892
  117.1 3.7 %copy-start.24 = (f32[512,1536]{1,0:T(8,128)S(1)}, f32[512,1536]{1,0:T(8,128)}, u32[]{:S(2)}) copy-start(f32[512,1536]{1,0:T(8,128)} %copy-done.23) | copy-start | bytes 9437188
  120.8 2.0 copy-start.19
  147.3 69.5 %reduce-scatter.5.cloned.1.call-start = ((), (), s32[]{:S(2)}) async-start(), calls=%async_computation.5 | async-start | bytes 7077888 | tf_op jit(solution)/shard_map/reduce_scatter | solution.py:505
  147.9 3.7 %copy-start.22 = (f32[128]{0:T(128)S(1)}, f32[128]{0:T(128)}, u32[]{:S(2)}) copy-start(f32[128]{0:T(128)} %copy-done.21) | copy-start | bytes 1540
  149.0 4.9 %copy-start.1 = (f32[12,128,128]{1,2,0:T(8,128)S(1)}, f32[12,128,128]{1,2,0:T(8,128)}, u32[]{:S(2)}) copy-start(f32[12,128,128]{1,2,0:T(8,128)} %get-tuple-element.58) | copy-start | bytes 2359300
  151.8 3.5 %copy-start.2 = (f32[12,128,128]{1,2,0:T(8,128)S(1)}, f32[12,128,128]{1,2,0:T(8,128)}, u32[]{:S(2)}) copy-start(f32[12,128,128]{1,2,0:T(8,128)} %get-tuple-element.58) | copy-start | bytes 2359300
  153.8 1.4 copy-start.11
  155.9 4.6 %copy-start.6 = (bf16[128,768]{0,1:T(8,128)(2,1)S(1)}, bf16[128,768]{0,1:T(8,128)(2,1)}, u32[]{:S(2)}) copy-start(bf16[128,768]{0,1:T(8,128)(2,1)} %copy-done.5) | copy-start | bytes 589828
  160.8 3.0 %copy-start.9 = (bf16[12,64,128]{2,1,0:T(8,128)(2,1)S(1)}, bf16[12,64,128]{2,1,0:T(8,128)(2,1)}, u32[]{:S(2)}) copy-start(bf16[12,64,128]{2,1,0:T(8,128)(2,1)} %copy-done.8) | copy-start | bytes 589828
  160.8 3.5 %copy-start.12 = (bf16[12,64,128]{2,1,0:T(8,128)(2,1)S(1)}, bf16[12,64,128]{2,1,0:T(8,128)(2,1)}, u32[]{:S(2)}) copy-start(bf16[12,64,128]{2,1,0:T(8,128)(2,1)} %convolution_convert_fusion.4) | copy-start | bytes 589828
  165.8 49.5 %copy-start.18 = (f32[128]{0:T(128)S(1)}, f32[128]{0:T(128)}, u32[]{:S(2)}) copy-start(f32[128]{0:T(128)} %copy-done.17) | copy-start | bytes 1540
Sparse Core Ops, SparseCore 0:
  9.6 13.6 all-gather.2
  24.8 12.2 all-gather.4
  147.4 11.4 reduce-scatter.2
  161.7 16.1 reduce-scatter.4
